TPU v7x, 32 devices: a whole 2x2x4 slice. The times are simulated.
32 devices in a mesh: req: 8 (over z, x), head: 4 (over y, core).
Axes of the slice: x: 2, y: 2, z: 4, core: 2. Of those that a mesh axis runs over, the one named last changes fastest.
Arguments:
- tokens: bfloat16 [8192, 1536], P(('req', 'head')), may hold values from -6 to 6
- norm1_gain: float32 [1536], replicated, may hold values from 0.1 to 1.9
- query_key_value_weight: bfloat16 [1536, 2048], replicated, may hold values from -0.15625 to 0.15625
- w_out: bfloat16 [1536, 1536], replicated, may hold values from -0.15625 to 0.15625
- norm2_gain: float32 [1536], replicated, may hold values from 0.1 to 1.9
- router_weight: float32 [1536, 8], replicated, may hold values from -0.078125 to 0.078125
- w_gate_up: bfloat16 [8, 1536, 1536], P('req'), may hold values from -0.15625 to 0.15625
- w_down: bfloat16 [8, 768, 1536], P('req'), may hold values from -0.21875 to 0.21875
- routes: int32 [8192, 4], P(('req', 'head')), may hold values from 0 to 7, all different within a row; in each aligned block of 256 rows (0 to 255, 256 to 511, ...) at most 192 rows name the same one
- key_page_store: bfloat16 [256, 128, 256], P('req'), may hold values from -100 to 100
- value_page_store: bfloat16 [256, 128, 256], P('req'), may hold values from -6 to 6
- page_table: int32 [16, 16], P('req'), may hold values from 0 to 31, as said below
- cached_pages: int32 [16], replicated, may hold values from 0 to 16
- anchor: int32 [16], replicated, may hold values from 0 to 15, as said below
Outputs:
- mixed: bfloat16 [8192, 1536], P(('req', 'head'))
- appended: bfloat16 [8192, 512], P(('req', 'head'))
Inputs may be any that keep to these rules, and one draw needn't show every extreme that they name: `page_table`: row o lists the pages of request o of the previous placement, as page numbers of the pool of index o // 2 of req; the rows of one index of req use distinct pages; entries past cached_pages[o] are not part of the cache. A permutation. Either anchor[i] = i, or request i and request anchor[i] lie on two indices of req that differ only in the lowest bit and trade places with each other; an index of req gives and takes at most one request.
All inputs are finite; a program needn't handle non-finite values.
Results may differ from a plain program's by a relative error of at most 0.011.
Values may be sent and summed in bfloat16 or wider, within the bound.
A program may use at most 128 MiB of HBM per device.

v0:
```python
import functools

import jax
import jax.numpy as jnp
from jax import lax
from jax.experimental import pallas as pl
from jax.experimental.pallas import tpu as pltpu
from jax.sharding import PartitionSpec as P

MODEL_WIDTH = 1536
QUERY_HEADS = 12
KEY_VALUE_HEADS = 2
HEAD_SIZE = 128
FE = 768
TOPK = 4
REQUEST_TOKENS = 512
LANES = 128
HALF = 64

EPS = 1e-06
THETA = 1000000.0
LOG2E = 1.4426950408889634
VMEM_LIMIT = 56 * 1024 * 1024
F32 = jnp.float32
BF16 = jnp.bfloat16


def swapped(value, axis, bit):
    mask = 2**bit
    pairs = [(source, source ^ mask) for source in range(lax.axis_size(axis))]
    return lax.ppermute(value, axis, pairs)


def params(*semantics):
    return pltpu.CompilerParams(
        vmem_limit_bytes=VMEM_LIMIT, dimension_semantics=("arbitrary",) * len(semantics)
    )


def project_kernel(n_groups, x_ref, gain_ref, w_ref, cos_ref, sin_ref, out_ref, app_ref, normed):
    step = pl.program_id(0)
    group_heads = QUERY_HEADS // n_groups
    share = n_groups // KEY_VALUE_HEADS
    width_q = group_heads * HEAD_SIZE

    @pl.when(step == 0)
    def _():
        x = x_ref[...].astype(F32)
        mean_sq = jnp.mean(x * x, axis=-1, keepdims=True)
        normed[...] = (x * lax.rsqrt(mean_sq + EPS) * gain_ref[...]).astype(BF16)

    rows = jnp.dot(normed[...], w_ref[...], preferred_element_type=F32)
    for at in range((QUERY_HEADS + 2 * KEY_VALUE_HEADS) // 2):

        @pl.when(step == at)
        def _(at=at):
            for part in range(2):
                head = 2 * at + part
                value = rows[:, part * HEAD_SIZE : (part + 1) * HEAD_SIZE]
                if head < QUERY_HEADS + KEY_VALUE_HEADS:
                    value = value * cos_ref[...] + pltpu.roll(value, HALF, 1) * sin_ref[...]
                value = value.astype(BF16)
                if head < QUERY_HEADS:
                    low = (head % group_heads) * HEAD_SIZE
                    out_ref[head // group_heads, :, low : low + HEAD_SIZE] = value
                else:
                    kind, kv = divmod(head - QUERY_HEADS, KEY_VALUE_HEADS)
                    low = width_q + kind * HEAD_SIZE
                    for group in range(kv * share, (kv + 1) * share):
                        out_ref[group, :, low : low + HEAD_SIZE] = value
                    low = (head - QUERY_HEADS) * HEAD_SIZE
                    app_ref[:, low : low + HEAD_SIZE] = value


def project(tokens, gain, weight, cosines, sines, n_groups):
    rows = tokens.shape[0]
    row_width = QUERY_HEADS // n_groups * HEAD_SIZE + 2 * HEAD_SIZE
    columns = weight.shape[1]
    tile = 2 * HEAD_SIZE
    whole = lambda *shape: pl.BlockSpec(shape, lambda j: (0,) * len(shape))
    return pl.pallas_call(
        functools.partial(project_kernel, n_groups),
        grid=(columns // tile,),
        in_specs=[
            whole(rows, MODEL_WIDTH),
            whole(1, MODEL_WIDTH),
            pl.BlockSpec((MODEL_WIDTH, tile), lambda j: (0, j)),
            whole(rows, LANES),
            whole(rows, LANES),
        ],
        out_specs=[
            whole(n_groups, rows, row_width),
            whole(rows, 2 * KEY_VALUE_HEADS * HEAD_SIZE),
        ],
        out_shape=[
            jax.ShapeDtypeStruct((n_groups, rows, row_width), BF16),
            jax.ShapeDtypeStruct((rows, 2 * KEY_VALUE_HEADS * HEAD_SIZE), BF16),
        ],
        scratch_shapes=[pltpu.VMEM((rows, MODEL_WIDTH), BF16)],
        compiler_params=params(0),
        cost_estimate=pl.CostEstimate(
            flops=2 * rows * MODEL_WIDTH * columns,
            bytes_accessed=2 * MODEL_WIDTH * columns,
            transcendentals=0,
        ),
        name="project",
    )(tokens, gain.reshape(1, -1), weight, cosines, sines)


def leave_kernel(pages_ref, k_ref, v_ref, out_ref, sems):
    count = out_ref.shape[1]
    column = pl.multiple_of(pages_ref[count] * HEAD_SIZE, HEAD_SIZE)
    copies = []
    for kind, pool in enumerate((k_ref, v_ref)):
        for at in range(count):
            copies.append(
                pltpu.make_async_copy(
                    pool.at[pages_ref[at], :, pl.ds(column, HEAD_SIZE)],
                    out_ref.at[kind, at],
                    sems.at[kind, at],
                )
            )
    for copy in copies:
        copy.start()
    for copy in copies:
        copy.wait()


def leaving_pages(pages, kv_index, k_store, v_store):
    count, page_size = pages.shape[0], k_store.shape[1]
    any_spec = pl.BlockSpec(memory_space=pl.ANY)
    return pl.pallas_call(
        leave_kernel,
        grid_spec=pltpu.PrefetchScalarGridSpec(
            num_scalar_prefetch=1,
            grid=(1,),
            in_specs=[any_spec, any_spec],
            out_specs=any_spec,
            scratch_shapes=[pltpu.SemaphoreType.DMA((2, count))],
        ),
        out_shape=jax.ShapeDtypeStruct((2, count, page_size, HEAD_SIZE), BF16),
        compiler_params=params(0),
        cost_estimate=pl.CostEstimate(
            flops=0, bytes_accessed=8 * count * page_size * HEAD_SIZE, transcendentals=0
        ),
        name="leaving",
    )(jnp.concatenate([pages, kv_index[None]]), k_store, v_store)


def attend_kernel(
    pages_ref, info_ref, rows_ref, k_ref, v_ref, got_ref, out_ref, kbuf, vbuf, top, total, acc, sems
):
    slot = pl.program_id(0)
    n_slots, span, _ = kbuf.shape
    page_size = k_ref.shape[1]
    group_heads = acc.shape[0]
    factor = HEAD_SIZE ** (-0.5) * LOG2E
    column = pl.multiple_of(info_ref[2 * n_slots] * HEAD_SIZE, HEAD_SIZE)
    width_q = group_heads * HEAD_SIZE

    def both(which, page, own):
        place = pl.ds(pl.multiple_of(page * page_size, page_size), page_size)
        pair = []
        for kind, (pool, buf) in enumerate(((k_ref, kbuf), (v_ref, vbuf))):
            if own:
                source = pool.at[pages_ref[which, page], :, pl.ds(column, HEAD_SIZE)]
            else:
                source = got_ref.at[kind, page]
            pair.append(
                pltpu.make_async_copy(source, buf.at[which, place, :], sems.at[which, page, kind])
            )
        return pair

    @pl.when(slot == 0)
    def _():
        for which in range(n_slots):

            @pl.when(info_ref[n_slots + which] == 0)
            def _(which=which):
                @pl.loop(0, info_ref[which])
                def _(page):
                    for copy in both(which, page, True):
                        copy.start()

            @pl.when(info_ref[n_slots + which] != 0)
            def _(which=which):
                @pl.loop(0, info_ref[which])
                def _(page):
                    for copy in both(which, page, False):
                        copy.start()

    keys_t = (((1,), (1,)), ((), ()))
    values_t = (((0,), (0,)), ((), ()))

    def query(head):
        return rows_ref[0, :, head * HEAD_SIZE : (head + 1) * HEAD_SIZE]

    fresh_k = rows_ref[0, :, width_q : width_q + HEAD_SIZE]
    fresh_v = rows_ref[0, :, width_q + HEAD_SIZE : width_q + 2 * HEAD_SIZE]
    tokens = rows_ref.shape[1]
    key_pos = lax.broadcasted_iota(jnp.int32, (tokens, tokens), 0)
    query_pos = lax.broadcasted_iota(jnp.int32, (tokens, tokens), 1)
    for head in range(group_heads):
        scores = lax.dot_general(fresh_k, query(head), keys_t, preferred_element_type=F32)
        scores = jnp.where(key_pos <= query_pos, scores, -jnp.inf)
        largest = jnp.max(scores, axis=0, keepdims=True)
        weights = jnp.exp2((scores - largest) * factor)
        top[head] = largest
        total[head] = jnp.sum(weights, axis=0, keepdims=True)
        acc[head] = lax.dot_general(
            fresh_v, weights.astype(BF16), values_t, preferred_element_type=F32
        )

    def visit(first_page, n_pages):
        for step in range(n_pages):
            for copy in both(slot, first_page + step, True):
                copy.wait()
        place = pl.ds(pl.multiple_of(first_page * page_size, page_size), n_pages * page_size)
        keys = kbuf[slot, place, :]
        values = vbuf[slot, place, :]
        for head in range(group_heads):
            scores = lax.dot_general(keys, query(head), keys_t, preferred_element_type=F32)
            old = top[head]
            largest = jnp.maximum(old, jnp.max(scores, axis=0, keepdims=True))
            fade = jnp.exp2((old - largest) * factor)
            weights = jnp.exp2((scores - largest) * factor)
            top[head] = largest
            total[head] = total[head] * fade + jnp.sum(weights, axis=0, keepdims=True)
            acc[head] = acc[head] * fade + lax.dot_general(
                values, weights.astype(BF16), values_t, preferred_element_type=F32
            )

    count = info_ref[slot]
    full = count // 4

    @pl.loop(0, full)
    def _(at):
        visit(at * 4, 4)

    @pl.loop(full * 4, count)
    def _(page):
        visit(page, 1)

    for head in range(group_heads):
        result = acc[head] / total[head]
        out_ref[0, :, head * HEAD_SIZE : (head + 1) * HEAD_SIZE] = result.T.astype(BF16)


def attend(pages, info, rows, k_store, v_store, got, group_heads):
    n_slots, maxp = pages.shape
    page_size = k_store.shape[1]
    span = maxp * page_size
    width = rows.shape[2]
    width_q = group_heads * HEAD_SIZE
    any_spec = pl.BlockSpec(memory_space=pl.ANY)
    return pl.pallas_call(
        attend_kernel,
        grid_spec=pltpu.PrefetchScalarGridSpec(
            num_scalar_prefetch=2,
            grid=(n_slots,),
            in_specs=[
                pl.BlockSpec((1, REQUEST_TOKENS, width), lambda s, *_: (s, 0, 0)),
                any_spec,
                any_spec,
                any_spec,
            ],
            out_specs=pl.BlockSpec((1, REQUEST_TOKENS, width_q), lambda s, *_: (s, 0, 0)),
            scratch_shapes=[
                pltpu.VMEM((n_slots, span, HEAD_SIZE), BF16),
                pltpu.VMEM((n_slots, span, HEAD_SIZE), BF16),
                pltpu.VMEM((group_heads, 1, REQUEST_TOKENS), F32),
                pltpu.VMEM((group_heads, 1, REQUEST_TOKENS), F32),
                pltpu.VMEM((group_heads, HEAD_SIZE, REQUEST_TOKENS), F32),
                pltpu.SemaphoreType.DMA((n_slots, maxp, 2)),
            ],
        ),
        out_shape=jax.ShapeDtypeStruct((n_slots, REQUEST_TOKENS, width_q), BF16),
        compiler_params=params(0),
        cost_estimate=pl.CostEstimate(
            flops=4 * n_slots * span * REQUEST_TOKENS * width_q,
            bytes_accessed=8 * n_slots * span * HEAD_SIZE,
            transcendentals=n_slots * span * REQUEST_TOKENS * group_heads,
        ),
        name="attend",
    )(pages, info, rows, k_store, v_store, got)


def settle_kernel(x_ref, back_ref, w_ref, gain_ref, router_ref, routes_ref, res_ref, out_ref):
    step = pl.program_id(0)
    product = jnp.dot(back_ref[0], w_ref[...], preferred_element_type=F32)

    @pl.when(step == 0)
    def _():
        res_ref[...] = x_ref[...].astype(F32) + product

    @pl.when(step > 0)
    def _():
        res_ref[...] += product

    @pl.when(step == pl.num_programs(0) - 1)
    def _():
        residual = res_ref[...]
        mean_sq = jnp.mean(residual * residual, axis=-1, keepdims=True)
        normed = (residual * lax.rsqrt(mean_sq + EPS) * gain_ref[...]).astype(BF16)
        out_ref[:, :MODEL_WIDTH] = normed
        logits = jnp.dot(
            normed.astype(F32),
            router_ref[...],
            precision=lax.Precision.HIGHEST,
            preferred_element_type=F32,
        )
        lane = lax.broadcasted_iota(jnp.int32, logits.shape, 1)
        named = lane == routes_ref[:, 0:1]
        for route in range(1, TOPK):
            named = named | (lane == routes_ref[:, route : route + 1])
        sigmoids = jnp.where(named, jax.nn.sigmoid(logits), 0.0)
        gates = sigmoids / jnp.sum(sigmoids, axis=1, keepdims=True)
        high = gates.astype(BF16).astype(F32)
        low = pltpu.roll(gates - high, HALF, 1)
        out_ref[:, MODEL_WIDTH:] = jnp.where(lane < HALF, high, low).astype(BF16)


def settle(tokens, back, w_out, gain, router, routes):
    rows = tokens.shape[0]
    n_groups, _, width_q = back.shape
    whole = lambda *shape: pl.BlockSpec(shape, lambda j: (0,) * len(shape))
    return pl.pallas_call(
        settle_kernel,
        grid=(n_groups,),
        in_specs=[
            whole(rows, MODEL_WIDTH),
            pl.BlockSpec((1, rows, width_q), lambda j: (j, 0, 0)),
            pl.BlockSpec((width_q, MODEL_WIDTH), lambda j: (j, 0)),
            whole(1, MODEL_WIDTH),
            whole(MODEL_WIDTH, LANES),
            whole(rows, TOPK),
        ],
        out_specs=[whole(rows, MODEL_WIDTH), whole(rows, MODEL_WIDTH + LANES)],
        out_shape=[
            jax.ShapeDtypeStruct((rows, MODEL_WIDTH), F32),
            jax.ShapeDtypeStruct((rows, MODEL_WIDTH + LANES), BF16),
        ],
        compiler_params=params(0),
        cost_estimate=pl.CostEstimate(
            flops=2 * rows * MODEL_WIDTH * MODEL_WIDTH,
            bytes_accessed=2 * MODEL_WIDTH * MODEL_WIDTH,
            transcendentals=0,
        ),
        name="settle",
    )(tokens, back, w_out, gain.reshape(1, -1), router, routes)


def expert_kernel(
    ids_ref, xa_ref, xb_ref, gate0, up0, down0, gate1, up1, down1, ya_ref, yb_ref, x, acc, mix
):
    which, part = pl.program_id(1), pl.program_id(2)
    half = xa_ref.shape[0]

    @pl.when((which == 0) & (part == 0))
    def _():
        x[:half] = xa_ref[...]
        x[half:] = xb_ref[...]

    def run(gate_w, up_w, down_w):
        rows = x[:, :MODEL_WIDTH]
        gate = jnp.dot(rows, gate_w[...], preferred_element_type=F32)
        up = jnp.dot(rows, up_w[...], preferred_element_type=F32)
        hidden = (jnp.maximum(gate, 0.0) * up).astype(BF16)
        product = jnp.dot(hidden, down_w[...], preferred_element_type=F32)

        @pl.when(part == 0)
        def _():
            acc[...] = product

        @pl.when(part > 0)
        def _():
            acc[...] += product

    @pl.when(which == 0)
    def _():
        run(gate0, up0, down0)

    @pl.when(which == 1)
    def _():
        run(gate1, up1, down1)

    @pl.when(part == pl.num_programs(2) - 1)
    def _():
        expert = ids_ref[which]
        extra = x[:, MODEL_WIDTH:].astype(F32)
        lane = lax.broadcasted_iota(jnp.int32, extra.shape, 1)
        mine = (lane == expert) | (lane == expert + HALF)
        gate = jnp.sum(jnp.where(mine, extra, 0.0), axis=1, keepdims=True)
        share = acc[...].astype(BF16).astype(F32) * gate

        @pl.when(which == 0)
        def _():
            mix[...] = share

        @pl.when(which == 1)
        def _():
            done = (mix[...] + share).astype(BF16)
            ya_ref[...] = done[:half]
            yb_ref[...] = done[half:]


def experts(ids, xa, xb, weights):
    half_rows, width = xa.shape
    half = min(half_rows, 256)
    tile = 256
    parts = FE // tile
    specs = []
    for which in range(2):
        at = (lambda e, f: jnp.where(e == 0, f, parts - 1)) if which == 0 else (
            lambda e, f: jnp.where(e == 0, 0, f)
        )
        specs += [
            pl.BlockSpec((MODEL_WIDTH, tile), lambda r, e, f, *_, at=at: (0, at(e, f))),
            pl.BlockSpec((MODEL_WIDTH, tile), lambda r, e, f, *_, at=at: (0, parts + at(e, f))),
            pl.BlockSpec((tile, MODEL_WIDTH), lambda r, e, f, *_, at=at: (at(e, f), 0)),
        ]
    row_spec = pl.BlockSpec((half, width), lambda r, e, f, *_: (r, 0))
    out_spec = pl.BlockSpec((half, MODEL_WIDTH), lambda r, e, f, *_: (r, 0))
    operands = []
    for gate_up, down in weights:
        operands += [gate_up, gate_up, down]
    return pl.pallas_call(
        expert_kernel,
        grid_spec=pltpu.PrefetchScalarGridSpec(
            num_scalar_prefetch=1,
            grid=(half_rows // half, 2, parts),
            in_specs=[row_spec, row_spec] + specs,
            out_specs=[out_spec, out_spec],
            scratch_shapes=[
                pltpu.VMEM((2 * half, width), BF16),
                pltpu.VMEM((2 * half, MODEL_WIDTH), F32),
                pltpu.VMEM((2 * half, MODEL_WIDTH), F32),
            ],
        ),
        out_shape=[jax.ShapeDtypeStruct((half_rows, MODEL_WIDTH), BF16)] * 2,
        compiler_params=params(0, 0, 0),
        cost_estimate=pl.CostEstimate(
            flops=24 * half_rows * MODEL_WIDTH * FE,
            bytes_accessed=12 * MODEL_WIDTH * FE,
            transcendentals=0,
        ),
        name="experts",
    )(ids, xa, xb, *operands)


def mixture(ids, sent, weights, n_bits):
    half = sent.shape[0] // 2
    orders = (list(range(n_bits)), list(reversed(range(n_bits))))
    held = [[sent[:half]], [sent[half:]]]
    arrived = []
    for level in range(n_bits):
        pair = []
        for side in range(2):
            buffers = held[side]
            block = buffers[0] if len(buffers) == 1 else jnp.concatenate(buffers, axis=0)
            pair.append(swapped(block, "req", orders[side][level]))
        for side in range(2):
            held[side].append(pair[side])
        arrived.append(pair)
    own = experts(ids, held[0][0], held[1][0], weights)
    outcome = [experts(ids, pair[0], pair[1], weights) for pair in arrived]
    totals = []
    for side in range(2):
        added = [own[side].astype(F32)]
        waiting = [outcome[level][side].astype(F32) for level in range(n_bits)]
        for level in reversed(range(n_bits)):
            back = swapped(waiting[level].astype(BF16), "req", orders[side][level]).astype(F32)
            added.append(back[:half])
            low = half
            for below in range(level):
                size = half * 2**below
                waiting[below] = waiting[below] + back[low : low + size]
                low += size
        totals.append(functools.reduce(jnp.add, added))
    return jnp.concatenate(totals, axis=0)


def on_device(
    tokens,
    norm1_gain,
    query_key_value_weight,
    w_out,
    norm2_gain,
    router_weight,
    w_gate_up,
    w_down,
    routes,
    key_page_store,
    value_page_store,
    page_table,
    cached_pages,
    anchor,
):
    req_index = lax.axis_index("req")
    head_index = lax.axis_index("head")
    n_groups = lax.axis_size("head")
    req_count = lax.axis_size("req")
    rows = tokens.shape[0]
    req_dev = page_table.shape[0]
    page_size = key_page_store.shape[1]
    group_heads = QUERY_HEADS // n_groups
    kv_index = head_index // (n_groups // KEY_VALUE_HEADS)
    far_bit = req_count.bit_length() - 2
    far_mask = 2**far_bit

    partner = req_index ^ 1
    partner_anchor = lax.dynamic_slice_in_dim(anchor, partner * req_dev, req_dev, 0)
    leaving = partner_anchor // req_dev == req_index
    out_row = jnp.sum(jnp.where(leaving, partner_anchor, 0)) % req_dev
    out_pages = lax.dynamic_index_in_dim(page_table, out_row, 0, keepdims=False)
    got = swapped(leaving_pages(out_pages, kv_index, key_page_store, value_page_store), "req", 0)

    gate_rows = w_gate_up.shape[1] // n_groups
    down_rows = w_down.shape[1] // n_groups
    gate_share = lax.dynamic_slice_in_dim(w_gate_up[0], head_index * gate_rows, gate_rows, 0)
    down_share = lax.dynamic_slice_in_dim(w_down[0], head_index * down_rows, down_rows, 0)
    gate_share = swapped(gate_share, "req", far_bit)
    down_share = swapped(down_share, "req", far_bit)
    far_gate_up = lax.all_gather(gate_share, "head", axis=0, tiled=True)
    far_down = lax.all_gather(down_share, "head", axis=0, tiled=True)

    row_ids = (req_index * n_groups + head_index) * rows + jnp.arange(rows, dtype=jnp.int32)
    request = row_ids // REQUEST_TOKENS
    positions = cached_pages[anchor[request]] * page_size + row_ids % REQUEST_TOKENS
    frequency = jnp.exp(
        -jnp.log(F32(THETA)) * jnp.arange(HALF, dtype=F32) * 2.0 / HEAD_SIZE
    )
    angles = positions.astype(F32)[:, None] * frequency[None, :]
    cosine, sine = jnp.cos(angles), jnp.sin(angles)
    outgoing, appended = project(
        tokens,
        norm1_gain,
        query_key_value_weight,
        jnp.concatenate([cosine, cosine], axis=1),
        jnp.concatenate([-sine, sine], axis=1),
        n_groups,
    )
    head_rows = lax.all_to_all(outgoing, "head", split_axis=0, concat_axis=0, tiled=True)
    head_rows = head_rows.reshape(req_dev, REQUEST_TOKENS, outgoing.shape[2])

    slot_anchor = lax.dynamic_slice_in_dim(anchor, req_index * req_dev, req_dev, 0)
    moved = (slot_anchor // req_dev != req_index).astype(jnp.int32)
    pages = page_table[slot_anchor % req_dev]
    info = jnp.concatenate([cached_pages[slot_anchor], moved, kv_index[None].astype(jnp.int32)])
    answers = attend(pages, info, head_rows, key_page_store, value_page_store, got, group_heads)
    answers = answers.reshape(n_groups, rows, group_heads * HEAD_SIZE)
    back = lax.all_to_all(answers, "head", split_axis=0, concat_axis=0, tiled=True)

    router = jnp.pad(router_weight, ((0, 0), (0, LANES - router_weight.shape[1])))
    residual, sent = settle(tokens, back, w_out, norm2_gain, router, routes)
    ids = jnp.stack([req_index, req_index ^ far_mask]).astype(jnp.int32)
    weights = ((w_gate_up[0], w_down[0]), (far_gate_up, far_down))
    mixed = (residual + mixture(ids, sent, weights, far_bit)).astype(BF16)
    return (mixed, appended)


def solution(mesh):
    return jax.shard_map(
        on_device,
        mesh=mesh,
        in_specs=(
            P(("req", "head"), None),
            P(),
            P(),
            P(),
            P(),
            P(),
            P("req", None, None),
            P("req", None, None),
            P(("req", "head"), None),
            P("req", None, None),
            P("req", None, None),
            P("req", None),
            P(),
            P(),
        ),
        out_specs=(P(("req", "head"), None), P(("req", "head"), None)),
        check_vma=False,
    )
```

profile of v0, /device:TPU:0, one launch (start us, length us, event | category | flops | bytes accessed | tf_op | source)
XLA Modules:
  0.0 326.0 jit_solution(9346205834503480074)
XLA Ops:
  7.2 1.1 dynamic-slice_bitcast_fusion.1
  8.3 4.1 %collective-permute-start.2 = (bf16[192,1536]{1,0:T(8,128)(2,1)S(1)}, bf16[192,1536]{1,0:T(8,128)(2,1)S(1)}, u32[]{:S(2)}, u32[]{:S(2)}) collective-permute-start(bf16[192,1536]{1,0:T(8,128)(2,1)S(1)} %dynamic-slice_bitcast_fusion.1), channel_id=1, source_target_pairs={{0,16},{4,20},{8,24},{12,28},{16,0},{20,4},{24,8},{28,12},{1,17},{... | collective-permute-start | bytes 1769480 | tf_op jit(solution)/shard_map/ppermute | solution.py:31
  12.4 26.0 %collective-permute-done.2 = bf16[192,1536]{1,0:T(8,128)(2,1)S(1)} collective-permute-done((bf16[192,1536]{1,0:T(8,128)(2,1)S(1)}, bf16[192,1536]{1,0:T(8,128)(2,1)S(1)}, u32[]{:S(2)}, u32[]{:S(2)}) %collective-permute-start.2) | collective-permute-done | bytes 589856 | tf_op jit(solution)/shard_map/ppermute | solution.py:31
  39.3 1.4 dynamic-slice_bitcast_fusion
  40.7 53.3 %collective-permute-done.1 = bf16[384,1536]{1,0:T(8,128)(2,1)S(1)} collective-permute-done((bf16[384,1536]{1,0:T(8,128)(2,1)S(1)}, bf16[384,1536]{1,0:T(8,128)(2,1)S(1)}, u32[]{:S(2)}, u32[]{:S(2)}) %collective-permute-start.1) | collective-permute-done | bytes 1179680 | tf_op jit(solution)/shard_map/ppermute | solution.py:31
  94.1 1.1 copy-done.9
  98.6 34.0 %leaving.1 = bf16[2,16,128,128]{3,2,1,0:T(8,128)(2,1)} custom-call(s32[17]{0:T(128)} %pad_add_fusion.1.pages_ref, bf16[32,128,256]{2,1,0:T(8,128)(2,1)} %k_ref.3, bf16[32,128,256]{2,1,0:T(8,128)(2,1)} %v_ref.3), custom_call_target="tpu_custom_call" | custom-call | bytes 2097152 | tf_op jit(solution)/shard_map/leaving/pallas_call | solution.py:132
  132.6 1.3 collective-permute-start
  135.4 4.2 %compare_select_fusion.8 = s32[256,1]{0,1:T(1,128)S(1)} fusion(s32[]{:T(128)} %bitcast.10, s32[]{:T(128)} %bitcast.11, s32[]{:T(128)} %bitcast.12, s32[]{:T(128)} %bitcast.13, s32[]{:T(128)} %bitcast.14, s32[]{:T(128)} %bitcast.16, s32[]{:T(128)} %bitcast.15, s32[]{:T(128)S(6)} %mul.48), kind=kLoop, calls=%fused_computation.49 | loop fusion | flops 7936 | bytes 1056 | tf_op jit(solution)/shard_map/gather | solution.py:529
  140.3 5.5 %select_select_fusion = s32[256]{0:T(256)S(1)} fusion(pred[256]{0:T(512)(128)(4,1)S(1)} %get-tuple-element.74, pred[256]{0:T(512)(128)(4,1)S(1)} %get-tuple-element.75, pred[256]{0:T(512)(128)(4,1)S(1)} %get-tuple-element.76, pred[256]{0:T(512)(128)(4,1)S(1)} %get-tuple-element.77, pred[256]{0:T(512)(128)(4,1)S(1)} %get-tuple-element.78, ...), kind=kLoop, calls=%fused_computation.78 | loop fusion | flops 2304 | bytes 4388 | tf_op jit(solution)/shard_map/gather | solution.py:529
  145.8 4.3 %compare_select_fusion.2 = (s32[256,1]{0,1:T(1,128)S(1)}, s32[256,1]{0,1:T(1,128)S(1)}) fusion(s32[]{:T(128)} %bitcast.28, s32[]{:T(128)} %bitcast.29, s32[]{:T(128)} %bitcast.30, s32[]{:T(128)} %bitcast.31, s32[]{:T(128)} %bitcast.32, s32[]{:T(128)} %bitcast.34, s32[]{:T(128)} %bitcast.33, s32[256,1]{0,1:T(1,128)S(1)} %bitcast.61), kind=kLoop, calls=%fused_computation.34 | loop fusion | flops 3840 | bytes 3100 | tf_op jit(solution)/shard_map/gather | solution.py:529
  150.2 5.4 %fusion.8 = f32[256]{0:T(256)S(1)} fusion(pred[256]{0:T(512)(128)(4,1)S(1)} %get-tuple-element.30, pred[256]{0:T(512)(128)(4,1)S(1)} %get-tuple-element.29, pred[256]{0:T(512)(128)(4,1)S(1)} %get-tuple-element.28, pred[256]{0:T(512)(128)(4,1)S(1)} %get-tuple-element.27, pred[256]{0:T(512)(128)(4,1)S(1)} %get-tuple-element.26, ...), kind=kLoop, calls=%fused_computation.79 | loop fusion | flops 6144 | bytes 4392 | tf_op jit(solution)/shard_map/convert_element_type | solution.py:533
  157.7 9.1 %project.1 = (bf16[4,256,640]{2,1,0:T(8,128)(2,1)}, bf16[256,512]{1,0:T(8,128)(2,1)}) custom-call(bf16[256,1536]{1,0:T(8,128)(2,1)} %x_ref.3, f32[1,1536]{1,0:T(1,128)} %reshape.115.gain_ref, bf16[1536,2048]{1,0:T(8,128)(2,1)} %w_ref.2, f32[256,128]{1,0:T(8,128)} %pad_maximum_fusion.2.cos_ref, f32[256,128]{1,0:T(8,128)} %pad_maximum_fusion.3.sin_ref), custom_call_target="tpu_custom_call" | custom-call | flops 1610612736 | bytes 6291456 | tf_op jit(solution)/shard_map/project/pallas_call | solution.py:81
  166.8 3.5 %all-to-all-start = ((bf16[4,256,640]{2,1,0:T(8,128)(2,1)}), bf16[4,256,640]{2,1,0:T(8,128)(2,1)S(1)}, u32[]{:S(2)}, u32[]{:S(2)}) async-start(bf16[4,256,640]{2,1,0:T(8,128)(2,1)} %get-tuple-element.12), calls=%async_computation | async-start | bytes 2621440 | tf_op jit(solution)/shard_map/all_to_all | solution.py:543
  171.0 1.1 gather_fusion
  172.8 14.8 %all-to-all-done = bf16[4,256,640]{2,1,0:T(8,128)(2,1)S(1)} async-done(((bf16[4,256,640]{2,1,0:T(8,128)(2,1)}), bf16[4,256,640]{2,1,0:T(8,128)(2,1)S(1)}, u32[]{:S(2)}, u32[]{:S(2)}) %all-to-all-start) | async-done | bytes 1310752 | tf_op jit(solution)/shard_map/all_to_all | solution.py:543
  187.6 1.1 copy-done.8
  189.0 15.0 %attend.1 = bf16[2,512,384]{2,1,0:T(8,128)(2,1)} custom-call(s32[2,16]{1,0:T(2,128)} %gather_fusion, s32[5]{0:T(128)} %pad_add_fusion.info_ref, bf16[2,512,640]{2,1,0:T(8,128)(2,1)} %bitcast.57, bf16[32,128,256]{2,1,0:T(8,128)(2,1)} %k_ref.3, bf16[32,128,256]{2,1,0:T(8,128)(2,1)} %v_ref.3, bf16[2,16,128,128]{3,2,1,0:T(8,128)(2,1)} %copy-done.20), custom_call_target="tpu_custom_call" | custom-call | flops 3221225472 | bytes 4194304 | tf_op jit(solution)/shard_map/attend/pallas_call | solution.py:256
  204.1 3.8 %all-to-all-start.1 = ((bf16[4,256,384]{2,1,0:T(8,128)(2,1)}), bf16[4,256,384]{2,1,0:T(8,128)(2,1)S(1)}, u32[]{:S(2)}, u32[]{:S(2)}) async-start(bf16[4,256,384]{2,1,0:T(8,128)(2,1)} %bitcast.58), calls=%async_computation.1 | async-start | bytes 1572864 | tf_op jit(solution)/shard_map/all_to_all | solution.py:552
  210.5 8.8 %all-to-all-done.1.back_ref = bf16[4,256,384]{2,1,0:T(8,128)(2,1)S(1)} async-done(((bf16[4,256,384]{2,1,0:T(8,128)(2,1)}), bf16[4,256,384]{2,1,0:T(8,128)(2,1)S(1)}, u32[]{:S(2)}, u32[]{:S(2)}) %all-to-all-start.1) | async-done | bytes 786464 | tf_op jit(solution)/shard_map/all_to_all | solution.py:552
  220.2 8.7 %settle.1 = (f32[256,1536]{1,0:T(8,128)}, bf16[256,1664]{1,0:T(8,128)(2,1)}) custom-call(bf16[256,1536]{1,0:T(8,128)(2,1)} %x_ref.3, bf16[4,256,384]{2,1,0:T(8,128)(2,1)} %copy-done.4, bf16[1536,1536]{1,0:T(8,128)(2,1)} %w_ref.3, f32[1,1536]{1,0:T(1,128)} %reshape.118.gain_ref, f32[1536,128]{1,0:T(8,128)} %pad.4.router_ref, s32[256,4]{1,0:T(8,128)} %copy.19.routes_ref), custom_call_target="tpu_custom_call" | custom-call | flops 1207959552 | bytes 4718592 | tf_op jit(solution)/shard_map/settle/pallas_call | solution.py:327
  228.9 1.2 fusion.11
  230.2 1.9 collective-permute-start.3
  232.1 9.6 %collective-permute-done.3.xa_ref = bf16[128,1664]{1,0:T(8,128)(2,1)S(1)} collective-permute-done((bf16[128,1664]{1,0:T(8,128)(2,1)S(1)}, bf16[128,1664]{1,0:T(8,128)(2,1)S(1)}, u32[]{:S(2)}, u32[]{:S(2)}) %collective-permute-start.3) | collective-permute-done | bytes 426016 | tf_op jit(solution)/shard_map/ppermute | solution.py:31
  241.9 1.3 collective-permute-done.5.xb_ref
  244.9 16.7 %collective-permute-done.4.xa_ref = bf16[256,1664]{1,0:T(8,128)(2,1)S(1)} collective-permute-done((bf16[256,1664]{1,0:T(8,128)(2,1)S(1)}, bf16[256,1664]{1,0:T(8,128)(2,1)S(1)}, u32[]{:S(2)}, u32[]{:S(2)}) %collective-permute-start.4) | collective-permute-done | bytes 852000 | tf_op jit(solution)/shard_map/ppermute | solution.py:31
  261.6 1.1 collective-permute-done.6.xb_ref
  262.7 16.8 %experts.4 = (bf16[256,1536]{1,0:T(8,128)(2,1)}, bf16[256,1536]{1,0:T(8,128)(2,1)}) custom-call(s32[2]{0:T(128)} %pad_add_fusion.2.ids_ref, bf16[256,1664]{1,0:T(8,128)(2,1)} %copy-done.21, bf16[256,1664]{1,0:T(8,128)(2,1)} %collective-permute-done.6.xb_ref, bf16[1536,1536]{1,0:T(8,128)(2,1)} %bitcast.48, bf16[1536,1536]{1,0:T(8,128)(2,1)} %bitcast.49, ...), custom_call_target="tpu_custom_call" | custom-call | flops 7247757312 | bytes 14155776 | tf_op jit(solution)/shard_map/experts/pallas_call | solution.py:427
  280.5 1.6 collective-permute-start.9
  282.0 12.6 %experts.5 = (bf16[128,1536]{1,0:T(8,128)(2,1)}, bf16[128,1536]{1,0:T(8,128)(2,1)}) custom-call(s32[2]{0:T(128)} %pad_add_fusion.2.ids_ref, bf16[128,1664]{1,0:T(8,128)(2,1)} %copy-done.5, bf16[128,1664]{1,0:T(8,128)(2,1)} %copy-done.6, bf16[1536,1536]{1,0:T(8,128)(2,1)} %bitcast.50, bf16[1536,1536]{1,0:T(8,128)(2,1)} %bitcast.51, ...), custom_call_target="tpu_custom_call" | custom-call | flops 3623878656 | bytes 14155776 | tf_op jit(solution)/shard_map/experts/pallas_call | solution.py:427
  294.6 12.8 %experts.3 = (bf16[128,1536]{1,0:T(8,128)(2,1)}, bf16[128,1536]{1,0:T(8,128)(2,1)}) custom-call(s32[2]{0:T(128)} %pad_add_fusion.2.ids_ref, bf16[128,1664]{1,0:T(8,128)(2,1)} %copy-done.3, bf16[128,1664]{1,0:T(8,128)(2,1)} %copy-done.2, bf16[1536,1536]{1,0:T(8,128)(2,1)} %bitcast.52, bf16[1536,1536]{1,0:T(8,128)(2,1)} %bitcast.53, ...), custom_call_target="tpu_custom_call" | custom-call | flops 3623878656 | bytes 14155776 | tf_op jit(solution)/shard_map/experts/pallas_call | solution.py:427
  310.6 6.0 %collective-permute-done.8 = bf16[128,1536]{1,0:T(8,128)(2,1)S(1)} collective-permute-done((bf16[128,1536]{1,0:T(8,128)(2,1)S(1)}, bf16[128,1536]{1,0:T(8,128)(2,1)S(1)}, u32[]{:S(2)}, u32[]{:S(2)}) %collective-permute-start.8) | collective-permute-done | bytes 393248 | tf_op jit(solution)/shard_map/ppermute | solution.py:31
  (94 shorter events, 20.2 us)
Async XLA Ops:
  7.2 90.8 %copy-start = (s32[2,16]{1,0:T(2,128)S(1)}, s32[2,16]{1,0:T(2,128)}, u32[]{:S(2)}) copy-start(s32[2,16]{1,0:T(2,128)} %param.25) | copy-start | bytes 388
  7.2 255.6 %all-gather.5.cloned.1.call-start = ((), (), s32[]{:S(2)}) async-start(), calls=%async_computation.3 | async-start | bytes 2949120 | tf_op jit(solution)/shard_map/all_gather | solution.py:525
  8.3 30.1 %collective-permute-start.2 = (bf16[192,1536]{1,0:T(8,128)(2,1)S(1)}, bf16[192,1536]{1,0:T(8,128)(2,1)S(1)}, u32[]{:S(2)}, u32[]{:S(2)}) collective-permute-start(bf16[192,1536]{1,0:T(8,128)(2,1)S(1)} %dynamic-slice_bitcast_fusion.1), channel_id=1, source_target_pairs={{0,16},{4,20},{8,24},{12,28},{16,0},{20,4},{24,8},{28,12},{1,17},{... | collective-permute-start | bytes 1769480 | tf_op jit(solution)/shard_map/ppermute | solution.py:31
  39.2 223.5 %all-gather.3.cloned.1.call-start = ((), (), s32[]{:S(2)}) async-start(), calls=%async_computation.2 | async-start | bytes 5898240 | tf_op jit(solution)/shard_map/all_gather | solution.py:524
  39.3 55.9 %copy-start.15 = (s32[16]{0:T(128)S(1)}, s32[16]{0:T(128)}, u32[]{:S(2)}) copy-start(s32[16]{0:T(128)} %param.27) | copy-start | bytes 196
  40.7 53.4 %collective-permute-start.1 = (bf16[384,1536]{1,0:T(8,128)(2,1)S(1)}, bf16[384,1536]{1,0:T(8,128)(2,1)S(1)}, u32[]{:S(2)}, u32[]{:S(2)}) collective-permute-start(bf16[384,1536]{1,0:T(8,128)(2,1)S(1)} %dynamic-slice_bitcast_fusion), channel_id=1, source_target_pairs={{0,16},{4,20},{8,24},{12,28},{16,0},{20,4},{24,8},{28,12},{1,17},{... | collective-permute-start | bytes 3538952 | tf_op jit(solution)/shard_map/ppermute | solution.py:31
  94.1 1.1 copy-start.9
  98.6 35.3 %copy-start.17 = (f32[1536]{0:T(1024)S(1)}, f32[1536]{0:T(1024)}, u32[]{:S(2)}) copy-start(f32[1536]{0:T(1024)} %param.15) | copy-start | bytes 18436
  98.6 41.0 %copy-start.1 = (s32[16]{0:T(128)S(1)}, s32[16]{0:T(128)}, u32[]{:S(2)}) copy-start(s32[16]{0:T(128)} %param.26) | copy-start | bytes 196
  132.6 55.0 %collective-permute-start = (bf16[2,16,128,128]{3,2,1,0:T(8,128)(2,1)}, bf16[2,16,128,128]{3,2,1,0:T(8,128)(2,1)S(1)}, u32[]{:S(2)}, u32[]{:S(2)}) collective-permute-start(bf16[2,16,128,128]{3,2,1,0:T(8,128)(2,1)} %leaving.1), channel_id=1, source_target_pairs={{0,4},{4,0},{8,12},{12,8},{16,20},{20,16},{24,28},{28,24},{1,5},{5... | collective-permute-start | bytes 3145736 | tf_op jit(solution)/shard_map/ppermute | solution.py:31
  166.8 20.8 %all-to-all-start = ((bf16[4,256,640]{2,1,0:T(8,128)(2,1)}), bf16[4,256,640]{2,1,0:T(8,128)(2,1)S(1)}, u32[]{:S(2)}, u32[]{:S(2)}) async-start(bf16[4,256,640]{2,1,0:T(8,128)(2,1)} %get-tuple-element.12), calls=%async_computation | async-start | bytes 2621440 | tf_op jit(solution)/shard_map/all_to_all | solution.py:543
  187.6 1.4 copy-start.20
  204.1 3.9 %copy-start.18 = (f32[1536]{0:T(1024)S(1)}, f32[1536]{0:T(1024)}, u32[]{:S(2)}) copy-start(f32[1536]{0:T(1024)} %param.18) | copy-start | bytes 18436
  204.1 4.5 %copy-start.19 = (s32[256,4]{0,1:T(4,128)S(1)}, s32[256,4]{0,1:T(4,128)}, u32[]{:S(2)}) copy-start(s32[256,4]{0,1:T(4,128)} %param.22) | copy-start | bytes 12292
  204.1 5.2 %copy-start.16 = (f32[1536,8]{0,1:T(8,128)S(1)}, f32[1536,8]{0,1:T(8,128)}, u32[]{:S(2)}) copy-start(f32[1536,8]{0,1:T(8,128)} %param.19) | copy-start | bytes 147460
  204.1 15.3 %all-to-all-start.1 = ((bf16[4,256,384]{2,1,0:T(8,128)(2,1)}), bf16[4,256,384]{2,1,0:T(8,128)(2,1)S(1)}, u32[]{:S(2)}, u32[]{:S(2)}) async-start(bf16[4,256,384]{2,1,0:T(8,128)(2,1)} %bitcast.58), calls=%async_computation.1 | async-start | bytes 1572864 | tf_op jit(solution)/shard_map/all_to_all | solution.py:552
  230.1 13.1 %copy-start.2 = (bf16[128,1664]{1,0:T(8,128)(2,1)}, bf16[128,1664]{1,0:T(8,128)(2,1)S(1)}, u32[]{:S(2)}) copy-start(bf16[128,1664]{1,0:T(8,128)(2,1)S(1)} %get-tuple-element.35.xb_ref) | copy-start | bytes 1277956
  230.2 13.1 %copy-start.3 = (bf16[128,1664]{1,0:T(8,128)(2,1)}, bf16[128,1664]{1,0:T(8,128)(2,1)S(1)}, u32[]{:S(2)}) copy-start(bf16[128,1664]{1,0:T(8,128)(2,1)S(1)} %get-tuple-element.36.xa_ref) | copy-start | bytes 1277956
  230.2 11.6 %collective-permute-start.3 = (bf16[128,1664]{1,0:T(8,128)(2,1)S(1)}, bf16[128,1664]{1,0:T(8,128)(2,1)S(1)}, u32[]{:S(2)}, u32[]{:S(2)}) collective-permute-start(bf16[128,1664]{1,0:T(8,128)(2,1)S(1)} %get-tuple-element.36.xa_ref), channel_id=1, source_target_pairs={{0,4},{4,0},{8,12},{12,8},{16,20},{20,16},{24,28},{28,24},{1,5},{5... | collective-permute-start | bytes 1277960 | tf_op jit(solution)/shard_map/ppermute | solution.py:31
  232.1 11.1 %collective-permute-start.5 = (bf16[128,1664]{1,0:T(8,128)(2,1)S(1)}, bf16[128,1664]{1,0:T(8,128)(2,1)S(1)}, u32[]{:S(2)}, u32[]{:S(2)}) collective-permute-start(bf16[128,1664]{1,0:T(8,128)(2,1)S(1)} %get-tuple-element.35.xb_ref), channel_id=1, source_target_pairs={{0,8},{4,12},{8,0},{12,4},{16,24},{20,28},{24,16},{28,20},{1,9},{5... | collective-permute-start | bytes 1277960 | tf_op jit(solution)/shard_map/ppermute | solution.py:31
  241.7 1.6 copy-start.5
  241.8 19.8 %collective-permute-start.4 = (bf16[256,1664]{1,0:T(8,128)(2,1)S(1)}, bf16[256,1664]{1,0:T(8,128)(2,1)S(1)}, u32[]{:S(2)}, u32[]{:S(2)}) collective-permute-start(bf16[256,1664]{1,0:T(8,128)(2,1)S(1)} %pad_maximum_fusion), channel_id=1, source_target_pairs={{0,8},{4,12},{8,0},{12,4},{16,24},{20,28},{24,16},{28,20},{1,9},{5... | collective-permute-start | bytes 2555912 | tf_op jit(solution)/shard_map/ppermute | solution.py:31
  243.2 36.3 %copy-start.6 = (bf16[128,1664]{1,0:T(8,128)(2,1)}, bf16[128,1664]{1,0:T(8,128)(2,1)S(1)}, u32[]{:S(2)}) copy-start(bf16[128,1664]{1,0:T(8,128)(2,1)S(1)} %collective-permute-done.5.xb_ref) | copy-start | bytes 1277956
  243.3 19.5 %collective-permute-start.6 = (bf16[256,1664]{1,0:T(8,128)(2,1)S(1)}, bf16[256,1664]{1,0:T(8,128)(2,1)}, u32[]{:S(2)}, u32[]{:S(2)}) collective-permute-start(bf16[256,1664]{1,0:T(8,128)(2,1)S(1)} %pad_maximum_fusion.1), channel_id=1, source_target_pairs={{0,4},{4,0},{8,12},{12,8},{16,20},{20,16},{24,28},{28,24},{1,5},{5... | collective-permute-start | bytes 2555912 | tf_op jit(solution)/shard_map/ppermute | solution.py:31
  261.6 1.1 copy-start.21
  279.5 28.0 %collective-permute-start.7 = (bf16[256,1536]{1,0:T(8,128)(2,1)}, bf16[256,1536]{1,0:T(8,128)(2,1)S(1)}, u32[]{:S(2)}, u32[]{:S(2)}) collective-permute-start(bf16[256,1536]{1,0:T(8,128)(2,1)} %get-tuple-element.16), channel_id=1, source_target_pairs={{0,8},{4,12},{8,0},{12,4},{16,24},{20,28},{24,16},{28,20},{1,9},{5... | collective-permute-start | bytes 2359304 | tf_op jit(solution)/shard_map/ppermute | solution.py:31
  280.5 28.6 %collective-permute-start.9 = (bf16[256,1536]{1,0:T(8,128)(2,1)}, bf16[256,1536]{1,0:T(8,128)(2,1)S(1)}, u32[]{:S(2)}, u32[]{:S(2)}) collective-permute-start(bf16[256,1536]{1,0:T(8,128)(2,1)} %get-tuple-element.19), channel_id=1, source_target_pairs={{0,4},{4,0},{8,12},{12,8},{16,20},{20,16},{24,28},{28,24},{1,5},{5... | collective-permute-start | bytes 2359304 | tf_op jit(solution)/shard_map/ppermute | solution.py:31
  308.5 8.1 %copy-start.12 = (bf16[128,1536]{1,0:T(8,128)(2,1)S(1)}, bf16[128,1536]{1,0:T(8,128)(2,1)}, u32[]{:S(2)}) copy-start(bf16[128,1536]{1,0:T(8,128)(2,1)} %get-tuple-element.15) | copy-start | bytes 1179652
  308.5 8.1 %collective-permute-start.8 = (bf16[128,1536]{1,0:T(8,128)(2,1)S(1)}, bf16[128,1536]{1,0:T(8,128)(2,1)S(1)}, u32[]{:S(2)}, u32[]{:S(2)}) collective-permute-start(bf16[128,1536]{1,0:T(8,128)(2,1)S(1)} %fusion.3), channel_id=1, source_target_pairs={{0,4},{4,0},{8,12},{12,8},{16,20},{20,16},{24,28},{28,24},{1,5},{5... | collective-permute-start | bytes 1179656 | tf_op jit(solution)/shard_map/ppermute | solution.py:31
  309.6 8.1 %copy-start.11 = (bf16[128,1536]{1,0:T(8,128)(2,1)S(1)}, bf16[128,1536]{1,0:T(8,128)(2,1)}, u32[]{:S(2)}) copy-start(bf16[128,1536]{1,0:T(8,128)(2,1)} %get-tuple-element.18) | copy-start | bytes 1179652
  309.6 8.1 %collective-permute-start.10 = (bf16[128,1536]{1,0:T(8,128)(2,1)S(1)}, bf16[128,1536]{1,0:T(8,128)(2,1)S(1)}, u32[]{:S(2)}, u32[]{:S(2)}) collective-permute-start(bf16[128,1536]{1,0:T(8,128)(2,1)S(1)} %fusion.1), channel_id=1, source_target_pairs={{0,8},{4,12},{8,0},{12,4},{16,24},{20,28},{24,16},{28,20},{1,9},{5... | collective-permute-start | bytes 1179656 | tf_op jit(solution)/shard_map/ppermute | solution.py:31
  316.7 1.4 copy-start.7
  (5 other events, 4.8 us)
Sparse Core Ops, SparseCore 0:
  39.4 25.2 all-gather.4
  95.3 36.0 all-gather.2
where the time goes:
time: 328 us; the launch traced here: 326 us
  waiting for transfers between devices  139 us (42%)
  Pallas kernels  109 us (33%)
  other arithmetic  26.3 us (8%)
  starting transfers between devices  19.9 us (6%)
  between operations  16.4 us (5%)
  local copies, waits for them, and re-layouts  15.8 us (5%)
    ppermute x11, waiting for transfers between devices, swapped(): return lax.ppermute(value, axis, pairs)  115 us
    pallas_call x3, Pallas kernels, experts(): pl.pallas_call(expert_kernel, grid_spec=pltpu.PrefetchScalarGridSpec(num_...  42.2 us
    pallas_call x1, Pallas kernels, leaving_pages(): pl.pallas_call(leave_kernel, grid_spec=pltpu.PrefetchScalarGridSpec(num_s...  34 us
    pallas_call x1, Pallas kernels, attend(): pl.pallas_call(attend_kernel, grid_spec=pltpu.PrefetchScalarGridSpec(num_...  15 us
    all_to_all x1, waiting for transfers between devices, on_device(): lax.all_to_all(outgoing, 'head', split_axis=0, concat_axis=0, tiled=True)  14.8 us
    ppermute x11, starting transfers between devices, swapped(): return lax.ppermute(value, axis, pairs)  12.5 us
    gather x7, other arithmetic, on_device(): anchor[request]  9.84 us
    pallas_call x1, Pallas kernels, project(): pl.pallas_call(functools.partial(project_kernel, n_groups), grid=(columns...  9.13 us
  transfers between devices with their start and end apart: 15, of which 10 were waited for; matrix products, arithmetic and copies ran while one was open for 10% of the time, Pallas kernels for 28%

commit v1 on v0

--- a/solution.py
+++ b/solution.py
@@ -135,7 +135,9 @@
             num_scalar_prefetch=1,
             grid=(1,),
             in_specs=[any_spec, any_spec],
-            out_specs=any_spec,
+            out_specs=pl.BlockSpec(
+                (2, count, page_size, HEAD_SIZE), lambda *_: (0, 0, 0, 0)
+            ),
             scratch_shapes=[pltpu.SemaphoreType.DMA((2, count))],
         ),
         out_shape=jax.ShapeDtypeStruct((2, count, page_size, HEAD_SIZE), BF16),
@@ -148,7 +150,7 @@
 
 
 def attend_kernel(
-    pages_ref, info_ref, rows_ref, k_ref, v_ref, got_ref, out_ref, kbuf, vbuf, top, total, acc, sems
+    pages_ref, info_ref, rows_ref, k_ref, v_ref, got_ref, more_ref, out_ref, kbuf, vbuf, top, total, acc, sems
 ):
     slot = pl.program_id(0)
     n_slots, span, _ = kbuf.shape
@@ -158,14 +160,17 @@
     column = pl.multiple_of(info_ref[2 * n_slots] * HEAD_SIZE, HEAD_SIZE)
     width_q = group_heads * HEAD_SIZE
 
-    def both(which, page, own):
+    fetched = got_ref.shape[1]
+    mine = info_ref[2 * n_slots + 1]
+
+    def both(which, page, pool_of=None):
         place = pl.ds(pl.multiple_of(page * page_size, page_size), page_size)
         pair = []
         for kind, (pool, buf) in enumerate(((k_ref, kbuf), (v_ref, vbuf))):
-            if own:
+            if pool_of is None:
                 source = pool.at[pages_ref[which, page], :, pl.ds(column, HEAD_SIZE)]
             else:
-                source = got_ref.at[kind, page]
+                source = pool_of.at[kind, page % fetched]
             pair.append(
                 pltpu.make_async_copy(source, buf.at[which, place, :], sems.at[which, page, kind])
             )
@@ -179,15 +184,22 @@
             def _(which=which):
                 @pl.loop(0, info_ref[which])
                 def _(page):
-                    for copy in both(which, page, True):
+                    for copy in both(which, page):
                         copy.start()
 
             @pl.when(info_ref[n_slots + which] != 0)
             def _(which=which):
                 @pl.loop(0, info_ref[which])
                 def _(page):
-                    for copy in both(which, page, False):
-                        copy.start()
+                    @pl.when(page // fetched == mine)
+                    def _():
+                        for copy in both(which, page, got_ref):
+                            copy.start()
+
+                    @pl.when(page // fetched != mine)
+                    def _():
+                        for copy in both(which, page, more_ref):
+                            copy.start()
 
     keys_t = (((1,), (1,)), ((), ()))
     values_t = (((0,), (0,)), ((), ()))
@@ -213,7 +225,7 @@
 
     def visit(first_page, n_pages):
         for step in range(n_pages):
-            for copy in both(slot, first_page + step, True):
+            for copy in both(slot, first_page + step):
                 copy.wait()
         place = pl.ds(pl.multiple_of(first_page * page_size, page_size), n_pages * page_size)
         keys = kbuf[slot, place, :]
@@ -246,7 +258,7 @@
         out_ref[0, :, head * HEAD_SIZE : (head + 1) * HEAD_SIZE] = result.T.astype(BF16)
 
 
-def attend(pages, info, rows, k_store, v_store, got, group_heads):
+def attend(pages, info, rows, k_store, v_store, got, more, group_heads):
     n_slots, maxp = pages.shape
     page_size = k_store.shape[1]
     span = maxp * page_size
@@ -263,6 +275,7 @@
                 any_spec,
                 any_spec,
                 any_spec,
+                any_spec,
             ],
             out_specs=pl.BlockSpec((1, REQUEST_TOKENS, width_q), lambda s, *_: (s, 0, 0)),
             scratch_shapes=[
@@ -282,7 +295,7 @@
             transcendentals=n_slots * span * REQUEST_TOKENS * group_heads,
         ),
         name="attend",
-    )(pages, info, rows, k_store, v_store, got)
+    )(pages, info, rows, k_store, v_store, got, more)
 
 
 def settle_kernel(x_ref, back_ref, w_ref, gain_ref, router_ref, routes_ref, res_ref, out_ref):
@@ -351,7 +364,7 @@
 
 
 def expert_kernel(
-    ids_ref, xa_ref, xb_ref, gate0, up0, down0, gate1, up1, down1, ya_ref, yb_ref, x, acc, mix
+    ids_ref, xa_ref, xb_ref, gate0, up0, down0, gate1, up1, gate2, up2, down1, ya_ref, yb_ref, x, acc, mix
 ):
     which, part = pl.program_id(1), pl.program_id(2)
     half = xa_ref.shape[0]
@@ -361,10 +374,18 @@
         x[:half] = xa_ref[...]
         x[half:] = xb_ref[...]
 
+    def product_of(pieces):
+        total, low = None, 0
+        for piece in pieces:
+            depth = piece.shape[0]
+            term = jnp.dot(x[:, low : low + depth], piece[...], preferred_element_type=F32)
+            total = term if total is None else total + term
+            low += depth
+        return total
+
     def run(gate_w, up_w, down_w):
-        rows = x[:, :MODEL_WIDTH]
-        gate = jnp.dot(rows, gate_w[...], preferred_element_type=F32)
-        up = jnp.dot(rows, up_w[...], preferred_element_type=F32)
+        gate = product_of(gate_w)
+        up = product_of(up_w)
         hidden = (jnp.maximum(gate, 0.0) * up).astype(BF16)
         product = jnp.dot(hidden, down_w[...], preferred_element_type=F32)
 
@@ -378,11 +399,11 @@
 
     @pl.when(which == 0)
     def _():
-        run(gate0, up0, down0)
+        run((gate0,), (up0,), down0)
 
     @pl.when(which == 1)
     def _():
-        run(gate1, up1, down1)
+        run((gate1, gate2), (up1, up2), down1)
 
     @pl.when(part == pl.num_programs(2) - 1)
     def _():
@@ -409,21 +430,23 @@
     half = min(half_rows, 256)
     tile = 256
     parts = FE // tile
-    specs = []
-    for which in range(2):
-        at = (lambda e, f: jnp.where(e == 0, f, parts - 1)) if which == 0 else (
-            lambda e, f: jnp.where(e == 0, 0, f)
-        )
-        specs += [
-            pl.BlockSpec((MODEL_WIDTH, tile), lambda r, e, f, *_, at=at: (0, at(e, f))),
-            pl.BlockSpec((MODEL_WIDTH, tile), lambda r, e, f, *_, at=at: (0, parts + at(e, f))),
-            pl.BlockSpec((tile, MODEL_WIDTH), lambda r, e, f, *_, at=at: (at(e, f), 0)),
-        ]
+    specs, operands = [], []
+    for which, (gate_ups, down) in enumerate(weights):
+        if which == 0:
+            at = lambda e, f: jnp.where(e == 0, f, parts - 1)
+        else:
+            at = lambda e, f: jnp.where(e == 0, 0, f)
+        for gate_up in gate_ups:
+            shape = (gate_up.shape[0], tile)
+            specs += [
+                pl.BlockSpec(shape, lambda r, e, f, *_, at=at: (0, at(e, f))),
+                pl.BlockSpec(shape, lambda r, e, f, *_, at=at: (0, parts + at(e, f))),
+            ]
+            operands += [gate_up, gate_up]
+        specs.append(pl.BlockSpec((tile, MODEL_WIDTH), lambda r, e, f, *_, at=at: (at(e, f), 0)))
+        operands.append(down)
     row_spec = pl.BlockSpec((half, width), lambda r, e, f, *_: (r, 0))
     out_spec = pl.BlockSpec((half, MODEL_WIDTH), lambda r, e, f, *_: (r, 0))
-    operands = []
-    for gate_up, down in weights:
-        operands += [gate_up, gate_up, down]
     return pl.pallas_call(
         expert_kernel,
         grid_spec=pltpu.PrefetchScalarGridSpec(
@@ -462,12 +485,23 @@
         for side in range(2):
             held[side].append(pair[side])
         arrived.append(pair)
-    own = experts(ids, held[0][0], held[1][0], weights)
-    outcome = [experts(ids, pair[0], pair[1], weights) for pair in arrived]
+    early = experts(
+        ids,
+        jnp.concatenate(held[0][:-1], axis=0),
+        jnp.concatenate(held[1][:-1], axis=0),
+        weights,
+    )
+    early, last = lax.optimization_barrier((tuple(early), tuple(arrived[-1])))
+    late = experts(ids, last[0], last[1], weights)
     totals = []
     for side in range(2):
-        added = [own[side].astype(F32)]
-        waiting = [outcome[level][side].astype(F32) for level in range(n_bits)]
+        added = [early[side][:half].astype(F32)]
+        waiting, low = [], half
+        for level in range(n_bits - 1):
+            size = half * 2**level
+            waiting.append(early[side][low : low + size].astype(F32))
+            low += size
+        waiting.append(late[side].astype(F32))
         for level in reversed(range(n_bits)):
             back = swapped(waiting[level].astype(BF16), "req", orders[side][level]).astype(F32)
             added.append(back[:half])
@@ -513,20 +547,25 @@
     leaving = partner_anchor // req_dev == req_index
     out_row = jnp.sum(jnp.where(leaving, partner_anchor, 0)) % req_dev
     out_pages = lax.dynamic_index_in_dim(page_table, out_row, 0, keepdims=False)
-    got = swapped(leaving_pages(out_pages, kv_index, key_page_store, value_page_store), "req", 0)
-
-    gate_rows = w_gate_up.shape[1] // n_groups
-    down_rows = w_down.shape[1] // n_groups
-    gate_share = lax.dynamic_slice_in_dim(w_gate_up[0], head_index * gate_rows, gate_rows, 0)
-    down_share = lax.dynamic_slice_in_dim(w_down[0], head_index * down_rows, down_rows, 0)
-    gate_share = swapped(gate_share, "req", far_bit)
-    down_share = swapped(down_share, "req", far_bit)
-    far_gate_up = lax.all_gather(gate_share, "head", axis=0, tiled=True)
-    far_down = lax.all_gather(down_share, "head", axis=0, tiled=True)
-
-    row_ids = (req_index * n_groups + head_index) * rows + jnp.arange(rows, dtype=jnp.int32)
-    request = row_ids // REQUEST_TOKENS
-    positions = cached_pages[anchor[request]] * page_size + row_ids % REQUEST_TOKENS
+    half_pages = page_table.shape[1] // 2
+    core = head_index % 2
+    out_pages = lax.dynamic_slice_in_dim(out_pages, core * half_pages, half_pages, 0)
+    left = leaving_pages(out_pages, kv_index, key_page_store, value_page_store)
+    tokens, left = lax.optimization_barrier((tokens, left))
+    got = swapped(left, "req", 0)
+
+    def share_of(block):
+        count = block.shape[0] // n_groups
+        return lax.dynamic_slice_in_dim(block, head_index * count, count, 0)
+
+    middle = w_gate_up.shape[1] // 2
+    far_down = swapped(share_of(w_down[0]), "req", far_bit)
+    far_first = swapped(share_of(w_gate_up[0, :middle]), "req", far_bit)
+    far_second = swapped(share_of(w_gate_up[0, middle:]), "req", far_bit)
+
+    first_row = (req_index * n_groups + head_index) * rows
+    start = cached_pages[anchor[first_row // REQUEST_TOKENS]] * page_size
+    positions = start + first_row % REQUEST_TOKENS + jnp.arange(rows, dtype=jnp.int32)
     frequency = jnp.exp(
         -jnp.log(F32(THETA)) * jnp.arange(HALF, dtype=F32) * 2.0 / HEAD_SIZE
     )
@@ -540,21 +579,29 @@
         jnp.concatenate([-sine, sine], axis=1),
         n_groups,
     )
+    outgoing, got = lax.optimization_barrier((outgoing, got))
+    more = swapped(got, "head", 0)
     head_rows = lax.all_to_all(outgoing, "head", split_axis=0, concat_axis=0, tiled=True)
+    head_rows, far_down = lax.optimization_barrier((head_rows, far_down))
+    far_down = lax.all_gather(far_down, "head", axis=0, tiled=True)
     head_rows = head_rows.reshape(req_dev, REQUEST_TOKENS, outgoing.shape[2])
 
     slot_anchor = lax.dynamic_slice_in_dim(anchor, req_index * req_dev, req_dev, 0)
     moved = (slot_anchor // req_dev != req_index).astype(jnp.int32)
     pages = page_table[slot_anchor % req_dev]
-    info = jnp.concatenate([cached_pages[slot_anchor], moved, kv_index[None].astype(jnp.int32)])
-    answers = attend(pages, info, head_rows, key_page_store, value_page_store, got, group_heads)
+    info = jnp.concatenate([cached_pages[slot_anchor], moved, jnp.stack([kv_index, core]).astype(jnp.int32)])
+    answers = attend(pages, info, head_rows, key_page_store, value_page_store, got, more, group_heads)
     answers = answers.reshape(n_groups, rows, group_heads * HEAD_SIZE)
+    answers, far_first = lax.optimization_barrier((answers, far_first))
+    far_first = lax.all_gather(far_first, "head", axis=0, tiled=True)
     back = lax.all_to_all(answers, "head", split_axis=0, concat_axis=0, tiled=True)
 
     router = jnp.pad(router_weight, ((0, 0), (0, LANES - router_weight.shape[1])))
     residual, sent = settle(tokens, back, w_out, norm2_gain, router, routes)
+    sent, far_second = lax.optimization_barrier((sent, far_second))
+    far_second = lax.all_gather(far_second, "head", axis=0, tiled=True)
     ids = jnp.stack([req_index, req_index ^ far_mask]).astype(jnp.int32)
-    weights = ((w_gate_up[0], w_down[0]), (far_gate_up, far_down))
+    weights = (((w_gate_up[0],), w_down[0]), ((far_first, far_second), far_down))
     mixed = (residual + mixture(ids, sent, weights, far_bit)).astype(BF16)
     return (mixed, appended)
 

time: 328 us -> 232 us (0.71)
  waiting for transfers between devices: 139 us -> 91.4 us
  Pallas kernels: 109 us -> 71.1 us
  other arithmetic: 26.3 us -> 9.13 us
    ppermute x11 -> x13, waiting for transfers between devices: 115 us -> 36.4 us  [swapped(): return lax.ppermute(value, axis, pairs)]
    pallas_call x1, Pallas kernels: 34 us -> 2.73 us  [leaving_pages(): pl.pallas_call(leave_kernel, grid_spec=pltpu.PrefetchScalarGridSpec(num_s...]
    all_gather x2 -> x3, waiting for transfers between devices: 0.01 us -> 29.2 us  [the longest x1 26.2 us: on_device(): far_second = lax.all_gather(far_second, 'head', axis=0, tiled=True)]
    gather x9 -> x0, other arithmetic: 14.2 us -> none  [the longest x7 9.84 us: on_device(): anchor[request]]
    pallas_call x3 -> x2, Pallas kernels: 42.2 us -> 33.5 us  [experts(): pl.pallas_call(expert_kernel, grid_spec=pltpu.PrefetchScalarGridSpec(num_...]
    all_to_all x1, waiting for transfers between devices: 8.82 us -> 16.3 us  [on_device(): lax.all_to_all(answers, 'head', split_axis=0, concat_axis=0, tiled=True)]
    all_to_all x1, waiting for transfers between devices: 14.8 us -> 8.74 us  [on_device(): lax.all_to_all(outgoing, 'head', split_axis=0, concat_axis=0, tiled=True)]
    convert_element_type x1, other arithmetic: 5.45 us -> 0.01 us  [on_device(): angles = positions.astype(F32)[:, None] * frequency[None, :]]
  transfers between devices with their start and end apart: 15 -> 18, of which waited for: 10 -> 8; matrix products, arithmetic and copies ran while one was open for 10% -> 8% of each run, Pallas kernels for 28% -> 22%
where the time goes in v1:
time: 232 us; the launch traced here: 229 us
  waiting for transfers between devices  91.4 us (39%)
  Pallas kernels  71.1 us (31%)
  starting transfers between devices  22.6 us (10%)
  between operations  18.7 us (8%)
  local copies, waits for them, and re-layouts  16.4 us (7%)
  other arithmetic  9.13 us (4%)
    ppermute x13, waiting for transfers between devices, swapped(): return lax.ppermute(value, axis, pairs)  36.4 us
    pallas_call x2, Pallas kernels, experts(): pl.pallas_call(expert_kernel, grid_spec=pltpu.PrefetchScalarGridSpec(num_...  33.5 us
    all_gather x1, waiting for transfers between devices, on_device(): far_second = lax.all_gather(far_second, 'head', axis=0, tiled=True)  26.2 us
    pallas_call x1, Pallas kernels, attend(): pl.pallas_call(attend_kernel, grid_spec=pltpu.PrefetchScalarGridSpec(num_...  16.9 us
    all_to_all x1, waiting for transfers between devices, on_device(): lax.all_to_all(answers, 'head', split_axis=0, concat_axis=0, tiled=True)  16.3 us
    ppermute x13, starting transfers between devices, swapped(): return lax.ppermute(value, axis, pairs)  14.5 us
    pallas_call x1, Pallas kernels, project(): pl.pallas_call(functools.partial(project_kernel, n_groups), grid=(columns...  9.14 us
    pallas_call x1, Pallas kernels, settle(): pl.pallas_call(settle_kernel, grid=(n_groups,), in_specs=[whole(rows, MOD...  8.8 us
  transfers between devices with their start and end apart: 18, of which 8 were waited for; matrix products, arithmetic and copies ran while one was open for 8% of the time, Pallas kernels for 22%

profile of v1, /device:TPU:0, one launch (start us, length us, event | category | flops | bytes accessed | tf_op | source)
XLA Modules:
  0.0 229.2 jit_solution(220482692494589992)
XLA Ops:
  7.9 2.0 compare_select_fusion.3
  12.6 2.7 %leaving.1 = bf16[2,8,128,128]{3,2,1,0:T(8,128)(2,1)} custom-call(s32[9]{0:T(128)} %pad_add_fusion.pages_ref, bf16[32,128,256]{2,1,0:T(8,128)(2,1)} %k_ref.3, bf16[32,128,256]{2,1,0:T(8,128)(2,1)} %v_ref.3), custom_call_target="tpu_custom_call" | custom-call | bytes 1048576 | tf_op jit(solution)/shard_map/leaving/pallas_call | solution.py:132
  15.3 3.0 %collective-permute-start = (bf16[2,8,128,128]{3,2,1,0:T(8,128)(2,1)}, bf16[2,8,128,128]{3,2,1,0:T(8,128)(2,1)}, u32[]{:S(2)}, u32[]{:S(2)}) collective-permute-start(bf16[2,8,128,128]{3,2,1,0:T(8,128)(2,1)} %leaving.1), channel_id=1, source_target_pairs={{0,4},{4,0},{8,12},{12,8},{16,20},{20,16},{24,28},{28,24},{1,5},{5... | collective-permute-start | bytes 1572872 | tf_op jit(solution)/shard_map/ppermute | solution.py:31
  18.3 1.1 dynamic-slice_bitcast_fusion.2
  19.4 2.7 %collective-permute-start.1 = (bf16[192,1536]{1,0:T(8,128)(2,1)S(1)}, bf16[192,1536]{1,0:T(8,128)(2,1)S(1)}, u32[]{:S(2)}, u32[]{:S(2)}) collective-permute-start(bf16[192,1536]{1,0:T(8,128)(2,1)S(1)} %dynamic-slice_bitcast_fusion.2), channel_id=1, source_target_pairs={{0,16},{4,20},{8,24},{12,28},{16,0},{20,4},{24,8},{28,12},{1,17},{... | collective-permute-start | bytes 1769480 | tf_op jit(solution)/shard_map/ppermute | solution.py:31
  27.9 9.1 %project.1 = (bf16[4,256,640]{2,1,0:T(8,128)(2,1)}, bf16[256,512]{1,0:T(8,128)(2,1)}) custom-call(bf16[256,1536]{1,0:T(8,128)(2,1)} %x_ref.1, f32[1,1536]{1,0:T(1,128)} %reshape.32.gain_ref, bf16[1536,2048]{1,0:T(8,128)(2,1)} %w_ref.2, f32[256,128]{1,0:T(8,128)} %get-tuple-element.58.cos_ref, f32[256,128]{1,0:T(8,128)} %get-tuple-element.59.sin_ref), custom_call_target="tpu_custom_call" | custom-call | flops 1610612736 | bytes 6291456 | tf_op jit(solution)/shard_map/project/pallas_call | solution.py:81
  37.1 4.3 %all-to-all-start = ((bf16[4,256,640]{2,1,0:T(8,128)(2,1)}), bf16[4,256,640]{2,1,0:T(8,128)(2,1)}, u32[]{:S(2)}, u32[]{:S(2)}) async-start(bf16[4,256,640]{2,1,0:T(8,128)(2,1)} %get-tuple-element.27), calls=%async_computation | async-start | bytes 2621440 | tf_op jit(solution)/shard_map/all_to_all | solution.py:584
  41.4 2.7 %fusion.7 = (bf16[1,768,1536]{2,1,0:T(8,128)(2,1)S(1)}, bf16[1,768,1536]{2,1,0:T(8,128)(2,1)S(1)}) fusion(bf16[1,1536,1536]{2,1,0:T(8,128)(2,1)} %param.20), kind=kLoop, calls=%fused_computation.44 | loop fusion | bytes 9437184 | tf_op jit(solution)/shard_map/slice | solution.py:564
  45.8 1.1 gather_fusion
  47.5 1.1 gather_fusion.1
  48.6 1.3 pad_add_fusion.1.info_ref
  49.9 8.7 %all-to-all-done = bf16[4,256,640]{2,1,0:T(8,128)(2,1)} async-done(((bf16[4,256,640]{2,1,0:T(8,128)(2,1)}), bf16[4,256,640]{2,1,0:T(8,128)(2,1)}, u32[]{:S(2)}, u32[]{:S(2)}) %all-to-all-start) | async-done | bytes 1310752 | tf_op jit(solution)/shard_map/all_to_all | solution.py:584
  58.7 16.9 %attend.1 = bf16[2,512,384]{2,1,0:T(8,128)(2,1)} custom-call(s32[2,16]{1,0:T(2,128)} %gather_fusion, s32[6]{0:T(128)} %pad_add_fusion.1.info_ref, bf16[2,512,640]{2,1,0:T(8,128)(2,1)} %bitcast.6.rows_ref, bf16[32,128,256]{2,1,0:T(8,128)(2,1)} %k_ref.3, bf16[32,128,256]{2,1,0:T(8,128)(2,1)} %v_ref.3, bf16[2,8,128,128]{3,2,1,0:T(8,128)(2,1)} %collective-permute-done.got_ref, ...), custom_call_target="tpu_custom_call" | custom-call | flops 3221225472 | bytes 4194304 | tf_op jit(solution)/shard_map/attend/pallas_call | solution.py:268
  76.4 3.5 %all-to-all-start.1 = ((bf16[4,256,384]{2,1,0:T(8,128)(2,1)}), bf16[4,256,384]{2,1,0:T(8,128)(2,1)S(1)}, u32[]{:S(2)}, u32[]{:S(2)}) async-start(bf16[4,256,384]{2,1,0:T(8,128)(2,1)} %bitcast.22), calls=%async_computation.1 | async-start | bytes 1572864 | tf_op jit(solution)/shard_map/all_to_all | solution.py:597
  82.7 0.9 pad.4.router_ref
  83.7 16.3 %all-to-all-done.1.back_ref = bf16[4,256,384]{2,1,0:T(8,128)(2,1)S(1)} async-done(((bf16[4,256,384]{2,1,0:T(8,128)(2,1)}), bf16[4,256,384]{2,1,0:T(8,128)(2,1)S(1)}, u32[]{:S(2)}, u32[]{:S(2)}) %all-to-all-start.1) | async-done | bytes 786464 | tf_op jit(solution)/shard_map/all_to_all | solution.py:597
  100.9 8.8 %settle.1 = (f32[256,1536]{1,0:T(8,128)}, bf16[256,1664]{1,0:T(8,128)(2,1)}) custom-call(bf16[256,1536]{1,0:T(8,128)(2,1)} %x_ref.1, bf16[4,256,384]{2,1,0:T(8,128)(2,1)} %copy-done.2, bf16[1536,1536]{1,0:T(8,128)(2,1)} %w_ref.3, f32[1,1536]{1,0:T(1,128)} %reshape.35.gain_ref, f32[1536,128]{1,0:T(8,128)} %pad.4.router_ref, s32[256,4]{1,0:T(8,128)} %copy.19.routes_ref), custom_call_target="tpu_custom_call" | custom-call | flops 1207959552 | bytes 4718592 | tf_op jit(solution)/shard_map/settle/pallas_call | solution.py:340
  110.5 1.3 fusion.8
  112.0 10.9 %collective-permute-done.5 = bf16[128,1664]{1,0:T(8,128)(2,1)S(1)} collective-permute-done((bf16[128,1664]{1,0:T(8,128)(2,1)S(1)}, bf16[128,1664]{1,0:T(8,128)(2,1)S(1)}, u32[]{:S(2)}, u32[]{:S(2)}) %collective-permute-start.5) | collective-permute-done | bytes 426016 | tf_op jit(solution)/shard_map/ppermute | solution.py:31
  123.1 1.6 collective-permute-start.8
  125.3 2.9 %all-gather.8.cloned.1.call-done.down1 = bf16[768,1536]{1,0:T(8,128)(2,1)} async-done(((bf16[192,1536]{1,0:T(8,128)(2,1)}), bf16[768,1536]{1,0:T(8,128)(2,1)}) %all-gather.8.cloned.1.call-update) | async-done | bytes 2359312 | tf_op jit(solution)/shard_map/all_gather | solution.py:586
  128.3 26.2 %all-gather.6.cloned.1.call-done.gate2.up2 = bf16[768,1536]{1,0:T(8,128)(2,1)} async-done(((bf16[192,1536]{1,0:T(8,128)(2,1)}), bf16[768,1536]{1,0:T(8,128)(2,1)}) %all-gather.6.cloned.1.call-update) | async-done | bytes 2359312 | tf_op jit(solution)/shard_map/all_gather | solution.py:602
  154.5 16.7 %experts.2 = (bf16[256,1536]{1,0:T(8,128)(2,1)}, bf16[256,1536]{1,0:T(8,128)(2,1)}) custom-call(s32[2]{0:T(128)} %pad_add_fusion.2.ids_ref, bf16[256,1664]{1,0:T(8,128)(2,1)} %copy-done.4, bf16[256,1664]{1,0:T(8,128)(2,1)} %copy-done.5, bf16[1536,1536]{1,0:T(8,128)(2,1)} %bitcast.18, bf16[1536,1536]{1,0:T(8,128)(2,1)} %bitcast.19, ...), custom_call_target="tpu_custom_call" | custom-call | flops 7247757312 | bytes 14155776 | tf_op jit(solution)/shard_map/experts/pallas_call | solution.py:450
  172.4 16.8 %experts.3 = (bf16[256,1536]{1,0:T(8,128)(2,1)}, bf16[256,1536]{1,0:T(8,128)(2,1)}) custom-call(s32[2]{0:T(128)} %pad_add_fusion.2.ids_ref, bf16[256,1664]{1,0:T(8,128)(2,1)} %copy-done.16, bf16[256,1664]{1,0:T(8,128)(2,1)} %copy-done.17, bf16[1536,1536]{1,0:T(8,128)(2,1)} %bitcast.20, bf16[1536,1536]{1,0:T(8,128)(2,1)} %bitcast.21, ...), custom_call_target="tpu_custom_call" | custom-call | flops 7247757312 | bytes 14155776 | tf_op jit(solution)/shard_map/experts/pallas_call | solution.py:450
  189.2 1.5 collective-permute-start.11
  190.8 1.5 collective-permute-start.9
  192.3 16.9 %collective-permute-done.11 = bf16[256,1536]{1,0:T(8,128)(2,1)S(1)} collective-permute-done((bf16[256,1536]{1,0:T(8,128)(2,1)}, bf16[256,1536]{1,0:T(8,128)(2,1)S(1)}, u32[]{:S(2)}, u32[]{:S(2)}) %collective-permute-start.11) | collective-permute-done | bytes 786464 | tf_op jit(solution)/shard_map/ppermute | solution.py:31
  209.5 1.6 collective-permute-start.12
  211.3 1.5 collective-permute-start.10
  212.8 7.1 %collective-permute-done.12 = bf16[128,1536]{1,0:T(8,128)(2,1)S(1)} collective-permute-done((bf16[128,1536]{1,0:T(8,128)(2,1)S(1)}, bf16[128,1536]{1,0:T(8,128)(2,1)S(1)}, u32[]{:S(2)}, u32[]{:S(2)}) %collective-permute-start.12) | collective-permute-done | bytes 393248 | tf_op jit(solution)/shard_map/ppermute | solution.py:31
  220.1 1.4 collective-permute-done.10
  221.6 1.1 fusion
  (84 shorter events, 15.0 us)
Async XLA Ops:
  7.2 4.7 %copy-start = (s32[2,16]{1,0:T(2,128)S(1)}, s32[2,16]{1,0:T(2,128)}, u32[]{:S(2)}) copy-start(s32[2,16]{1,0:T(2,128)} %param.25) | copy-start | bytes 388
  12.6 9.5 %copy-start.13 = (s32[16]{0:T(128)S(1)}, s32[16]{0:T(128)}, u32[]{:S(2)}) copy-start(s32[16]{0:T(128)} %param.27) | copy-start | bytes 196
  12.6 12.0 %copy-start.1 = (s32[16]{0:T(128)S(1)}, s32[16]{0:T(128)}, u32[]{:S(2)}) copy-start(s32[16]{0:T(128)} %param.26) | copy-start | bytes 196
  12.6 13.3 %copy-start.11 = (f32[1536]{0:T(1024)S(1)}, f32[1536]{0:T(1024)}, u32[]{:S(2)}) copy-start(f32[1536]{0:T(1024)} %param.15) | copy-start | bytes 18436
  15.3 21.7 %collective-permute-start = (bf16[2,8,128,128]{3,2,1,0:T(8,128)(2,1)}, bf16[2,8,128,128]{3,2,1,0:T(8,128)(2,1)}, u32[]{:S(2)}, u32[]{:S(2)}) collective-permute-start(bf16[2,8,128,128]{3,2,1,0:T(8,128)(2,1)} %leaving.1), channel_id=1, source_target_pairs={{0,4},{4,0},{8,12},{12,8},{16,20},{20,16},{24,28},{28,24},{1,5},{5... | collective-permute-start | bytes 1572872 | tf_op jit(solution)/shard_map/ppermute | solution.py:31
  19.4 30.5 %collective-permute-start.1 = (bf16[192,1536]{1,0:T(8,128)(2,1)S(1)}, bf16[192,1536]{1,0:T(8,128)(2,1)S(1)}, u32[]{:S(2)}, u32[]{:S(2)}) collective-permute-start(bf16[192,1536]{1,0:T(8,128)(2,1)S(1)} %dynamic-slice_bitcast_fusion.2), channel_id=1, source_target_pairs={{0,16},{4,20},{8,24},{12,28},{16,0},{20,4},{24,8},{28,12},{1,17},{... | collective-permute-start | bytes 1769480 | tf_op jit(solution)/shard_map/ppermute | solution.py:31
  37.1 21.6 %all-to-all-start = ((bf16[4,256,640]{2,1,0:T(8,128)(2,1)}), bf16[4,256,640]{2,1,0:T(8,128)(2,1)}, u32[]{:S(2)}, u32[]{:S(2)}) async-start(bf16[4,256,640]{2,1,0:T(8,128)(2,1)} %get-tuple-element.27), calls=%async_computation | async-start | bytes 2621440 | tf_op jit(solution)/shard_map/all_to_all | solution.py:584
  41.4 84.0 %all-gather.4.cloned.1.call-start = ((), (), s32[]{:S(2)}) async-start(), calls=%async_computation.2 | async-start | bytes 2949120 | tf_op jit(solution)/shard_map/all_gather | solution.py:596
  41.4 4.4 %copy-start.15 = (s32[2]{0:T(128)S(1)}, s32[2]{0:T(128)}, u32[]{:S(2)}) copy-start(s32[2]{0:T(128)} %get-tuple-element.57) | copy-start | bytes 28
  44.1 14.6 %collective-permute-start.2 = (bf16[2,8,128,128]{3,2,1,0:T(8,128)(2,1)}, bf16[2,8,128,128]{3,2,1,0:T(8,128)(2,1)}, u32[]{:S(2)}, u32[]{:S(2)}) collective-permute-start(bf16[2,8,128,128]{3,2,1,0:T(8,128)(2,1)} %collective-permute-done.got_ref), channel_id=1, source_target_pairs={{0,1},{1,0},{2,3},{3,2},{4,5},{5,4},{6,7},{7,6},{8,9},{9,8},{10,11... | collective-permute-start | bytes 1572872 | tf_op jit(solution)/shard_map/ppermute | solution.py:31
  45.4 30.2 %collective-permute-start.3 = (bf16[192,1536]{1,0:T(8,128)(2,1)}, bf16[192,1536]{1,0:T(8,128)(2,1)}, u32[]{:S(2)}, u32[]{:S(2)}) collective-permute-start(bf16[192,1536]{1,0:T(8,128)(2,1)} %dynamic-slice_bitcast_fusion.1), channel_id=1, source_target_pairs={{0,16},{4,20},{8,24},{12,28},{16,0},{20,4},{24,8},{28,12},{1,17},{... | collective-permute-start | bytes 1769480 | tf_op jit(solution)/shard_map/ppermute | solution.py:31
  49.9 25.6 %copy-start.8 = (bf16[192,1536]{1,0:T(8,128)(2,1)}, bf16[192,1536]{1,0:T(8,128)(2,1)S(1)}, u32[]{:S(2)}) copy-start(bf16[192,1536]{1,0:T(8,128)(2,1)S(1)} %collective-permute-done.1) | copy-start | bytes 1769476
  75.6 5.4 %copy-start.12 = (f32[1536]{0:T(1024)S(1)}, f32[1536]{0:T(1024)}, u32[]{:S(2)}) copy-start(f32[1536]{0:T(1024)} %param.18) | copy-start | bytes 18436
  75.6 6.0 %copy-start.10 = (f32[1536,8]{0,1:T(8,128)S(1)}, f32[1536,8]{0,1:T(8,128)}, u32[]{:S(2)}) copy-start(f32[1536,8]{0,1:T(8,128)} %param.19) | copy-start | bytes 147460
  75.6 52.6 %all-gather.8.cloned.1.call-start = ((), (), s32[]{:S(2)}) async-start(), calls=%async_computation.4 | async-start | bytes 2949120 | tf_op jit(solution)/shard_map/all_gather | solution.py:586
  76.4 5.5 %copy-start.14 = (s32[256,4]{0,1:T(4,128)S(1)}, s32[256,4]{0,1:T(4,128)}, u32[]{:S(2)}) copy-start(s32[256,4]{0,1:T(4,128)} %param.22) | copy-start | bytes 12292
  76.4 23.6 %all-to-all-start.1 = ((bf16[4,256,384]{2,1,0:T(8,128)(2,1)}), bf16[4,256,384]{2,1,0:T(8,128)(2,1)S(1)}, u32[]{:S(2)}, u32[]{:S(2)}) async-start(bf16[4,256,384]{2,1,0:T(8,128)(2,1)} %bitcast.22), calls=%async_computation.1 | async-start | bytes 1572864 | tf_op jit(solution)/shard_map/all_to_all | solution.py:597
  79.9 74.6 %all-gather.6.cloned.1.call-start = ((), (), s32[]{:S(2)}) async-start(), calls=%async_computation.3 | async-start | bytes 2949120 | tf_op jit(solution)/shard_map/all_gather | solution.py:602
  81.1 28.6 %collective-permute-start.4 = (bf16[192,1536]{1,0:T(8,128)(2,1)}, bf16[192,1536]{1,0:T(8,128)(2,1)S(1)}, u32[]{:S(2)}, u32[]{:S(2)}) collective-permute-start(bf16[192,1536]{1,0:T(8,128)(2,1)} %dynamic-slice_bitcast_fusion), channel_id=1, source_target_pairs={{0,16},{4,20},{8,24},{12,28},{16,0},{20,4},{24,8},{28,12},{1,17},{... | collective-permute-start | bytes 1769480 | tf_op jit(solution)/shard_map/ppermute | solution.py:31
  111.8 11.1 %collective-permute-start.5 = (bf16[128,1664]{1,0:T(8,128)(2,1)S(1)}, bf16[128,1664]{1,0:T(8,128)(2,1)S(1)}, u32[]{:S(2)}, u32[]{:S(2)}) collective-permute-start(bf16[128,1664]{1,0:T(8,128)(2,1)S(1)} %get-tuple-element.51), channel_id=1, source_target_pairs={{0,4},{4,0},{8,12},{12,8},{16,20},{20,16},{24,28},{28,24},{1,5},{5... | collective-permute-start | bytes 1277960 | tf_op jit(solution)/shard_map/ppermute | solution.py:31
  111.9 11.1 %collective-permute-start.6 = (bf16[128,1664]{1,0:T(8,128)(2,1)S(1)}, bf16[128,1664]{1,0:T(8,128)(2,1)S(1)}, u32[]{:S(2)}, u32[]{:S(2)}) collective-permute-start(bf16[128,1664]{1,0:T(8,128)(2,1)S(1)} %get-tuple-element.50), channel_id=1, source_target_pairs={{0,8},{4,12},{8,0},{12,4},{16,24},{20,28},{24,16},{28,20},{1,9},{5... | collective-permute-start | bytes 1277960 | tf_op jit(solution)/shard_map/ppermute | solution.py:31
  122.9 31.6 %copy-start.4 = (bf16[256,1664]{1,0:T(8,128)(2,1)}, bf16[256,1664]{1,0:T(8,128)(2,1)S(1)}, u32[]{:S(2)}) copy-start(bf16[256,1664]{1,0:T(8,128)(2,1)S(1)} %pad_maximum_fusion.xa_ref) | copy-start | bytes 2555908
  122.9 48.3 %collective-permute-start.7 = (bf16[256,1664]{1,0:T(8,128)(2,1)S(1)}, bf16[256,1664]{1,0:T(8,128)(2,1)S(1)}, u32[]{:S(2)}, u32[]{:S(2)}) collective-permute-start(bf16[256,1664]{1,0:T(8,128)(2,1)S(1)} %pad_maximum_fusion.xa_ref), channel_id=1, source_target_pairs={{0,8},{4,12},{8,0},{12,4},{16,24},{20,28},{24,16},{28,20},{1,9},{5... | collective-permute-start | bytes 2555912 | tf_op jit(solution)/shard_map/ppermute | solution.py:31
  123.1 31.4 %copy-start.5 = (bf16[256,1664]{1,0:T(8,128)(2,1)}, bf16[256,1664]{1,0:T(8,128)(2,1)S(1)}, u32[]{:S(2)}) copy-start(bf16[256,1664]{1,0:T(8,128)(2,1)S(1)} %pad_maximum_fusion.1.xb_ref) | copy-start | bytes 2555908
  123.1 48.2 %collective-permute-start.8 = (bf16[256,1664]{1,0:T(8,128)(2,1)S(1)}, bf16[256,1664]{1,0:T(8,128)(2,1)S(1)}, u32[]{:S(2)}, u32[]{:S(2)}) collective-permute-start(bf16[256,1664]{1,0:T(8,128)(2,1)S(1)} %pad_maximum_fusion.1.xb_ref), channel_id=1, source_target_pairs={{0,4},{4,0},{8,12},{12,8},{16,20},{20,16},{24,28},{28,24},{1,5},{5... | collective-permute-start | bytes 2555912 | tf_op jit(solution)/shard_map/ppermute | solution.py:31
  189.2 20.2 %copy-start.7 = (bf16[256,1536]{1,0:T(8,128)(2,1)S(1)}, bf16[256,1536]{1,0:T(8,128)(2,1)}, u32[]{:S(2)}) copy-start(bf16[256,1536]{1,0:T(8,128)(2,1)} %get-tuple-element.43) | copy-start | bytes 2359300
  189.2 20.0 %collective-permute-start.11 = (bf16[256,1536]{1,0:T(8,128)(2,1)}, bf16[256,1536]{1,0:T(8,128)(2,1)S(1)}, u32[]{:S(2)}, u32[]{:S(2)}) collective-permute-start(bf16[256,1536]{1,0:T(8,128)(2,1)} %get-tuple-element.44), channel_id=1, source_target_pairs={{0,4},{4,0},{8,12},{12,8},{16,20},{20,16},{24,28},{28,24},{1,5},{5... | collective-permute-start | bytes 2359304 | tf_op jit(solution)/shard_map/ppermute | solution.py:31
  190.8 20.3 %collective-permute-start.9 = (bf16[256,1536]{1,0:T(8,128)(2,1)}, bf16[256,1536]{1,0:T(8,128)(2,1)S(1)}, u32[]{:S(2)}, u32[]{:S(2)}) collective-permute-start(bf16[256,1536]{1,0:T(8,128)(2,1)} %get-tuple-element.42), channel_id=1, source_target_pairs={{0,8},{4,12},{8,0},{12,4},{16,24},{20,28},{24,16},{28,20},{1,9},{5... | collective-permute-start | bytes 2359304 | tf_op jit(solution)/shard_map/ppermute | solution.py:31
  209.4 1.8 copy-start.6
  209.5 10.5 %collective-permute-start.12 = (bf16[128,1536]{1,0:T(8,128)(2,1)S(1)}, bf16[128,1536]{1,0:T(8,128)(2,1)S(1)}, u32[]{:S(2)}, u32[]{:S(2)}) collective-permute-start(bf16[128,1536]{1,0:T(8,128)(2,1)S(1)} %fusion.1), channel_id=1, source_target_pairs={{0,8},{4,12},{8,0},{12,4},{16,24},{20,28},{24,16},{28,20},{1,9},{5... | collective-permute-start | bytes 1179656 | tf_op jit(solution)/shard_map/ppermute | solution.py:31
  211.3 10.2 %collective-permute-start.10 = (bf16[128,1536]{1,0:T(8,128)(2,1)S(1)}, bf16[128,1536]{1,0:T(8,128)(2,1)S(1)}, u32[]{:S(2)}, u32[]{:S(2)}) collective-permute-start(bf16[128,1536]{1,0:T(8,128)(2,1)S(1)} %fusion.3), channel_id=1, source_target_pairs={{0,4},{4,0},{8,12},{12,8},{16,20},{20,16},{24,28},{28,24},{1,5},{5... | collective-permute-start | bytes 1179656 | tf_op jit(solution)/shard_map/ppermute | solution.py:31
  220.1 1.5 copy-start.3
  (4 other events, 3.8 us)
Sparse Core Ops, SparseCore 0:
  75.7 29.9 all-gather.3
  107.3 20.9 all-gather.7
  130.4 24.0 all-gather.5

commit v2 on v1

--- a/solution.py
+++ b/solution.py
@@ -363,9 +363,8 @@
     )(tokens, back, w_out, gain.reshape(1, -1), router, routes)
 
 
-def expert_kernel(
-    ids_ref, xa_ref, xb_ref, gate0, up0, down0, gate1, up1, gate2, up2, down1, ya_ref, yb_ref, x, acc, mix
-):
+def expert_kernel(layout, ids_ref, xa_ref, xb_ref, *refs):
+    ya_ref, yb_ref, x, acc, mix = refs[-5:]
     which, part = pl.program_id(1), pl.program_id(2)
     half = xa_ref.shape[0]
 
@@ -397,13 +396,14 @@
         def _():
             acc[...] += product
 
-    @pl.when(which == 0)
-    def _():
-        run((gate0,), (up0,), down0)
-
-    @pl.when(which == 1)
-    def _():
-        run((gate1, gate2), (up1, up2), down1)
+    low = 0
+    for place, pieces in enumerate(layout):
+        own = refs[low : low + 2 * pieces + 1]
+        low += 2 * pieces + 1
+
+        @pl.when(which == place)
+        def _(own=own):
+            run(own[:-1:2], own[1:-1:2], own[-1])
 
     @pl.when(part == pl.num_programs(2) - 1)
     def _():
@@ -414,13 +414,15 @@
         gate = jnp.sum(jnp.where(mine, extra, 0.0), axis=1, keepdims=True)
         share = acc[...].astype(BF16).astype(F32) * gate
 
-        @pl.when(which == 0)
+        if len(layout) == 2:
+
+            @pl.when(which == 0)
+            def _():
+                mix[...] = share
+
+        @pl.when(which == len(layout) - 1)
         def _():
-            mix[...] = share
-
-        @pl.when(which == 1)
-        def _():
-            done = (mix[...] + share).astype(BF16)
+            done = (mix[...] + share if len(layout) == 2 else share).astype(BF16)
             ya_ref[...] = done[:half]
             yb_ref[...] = done[half:]
 
@@ -432,7 +434,9 @@
     parts = FE // tile
     specs, operands = [], []
     for which, (gate_ups, down) in enumerate(weights):
-        if which == 0:
+        if len(weights) == 1:
+            at = lambda e, f: f
+        elif which == 0:
             at = lambda e, f: jnp.where(e == 0, f, parts - 1)
         else:
             at = lambda e, f: jnp.where(e == 0, 0, f)
@@ -448,10 +452,10 @@
     row_spec = pl.BlockSpec((half, width), lambda r, e, f, *_: (r, 0))
     out_spec = pl.BlockSpec((half, MODEL_WIDTH), lambda r, e, f, *_: (r, 0))
     return pl.pallas_call(
-        expert_kernel,
+        functools.partial(expert_kernel, tuple(len(pieces) for pieces, _ in weights)),
         grid_spec=pltpu.PrefetchScalarGridSpec(
             num_scalar_prefetch=1,
-            grid=(half_rows // half, 2, parts),
+            grid=(half_rows // half, len(weights), parts),
             in_specs=[row_spec, row_spec] + specs,
             out_specs=[out_spec, out_spec],
             scratch_shapes=[
@@ -463,8 +467,8 @@
         out_shape=[jax.ShapeDtypeStruct((half_rows, MODEL_WIDTH), BF16)] * 2,
         compiler_params=params(0, 0, 0),
         cost_estimate=pl.CostEstimate(
-            flops=24 * half_rows * MODEL_WIDTH * FE,
-            bytes_accessed=12 * MODEL_WIDTH * FE,
+            flops=12 * len(weights) * half_rows * MODEL_WIDTH * FE,
+            bytes_accessed=6 * len(weights) * MODEL_WIDTH * FE,
             transcendentals=0,
         ),
         name="experts",
@@ -485,21 +489,20 @@
         for side in range(2):
             held[side].append(pair[side])
         arrived.append(pair)
-    early = experts(
-        ids,
-        jnp.concatenate(held[0][:-1], axis=0),
-        jnp.concatenate(held[1][:-1], axis=0),
-        weights,
-    )
-    early, last = lax.optimization_barrier((tuple(early), tuple(arrived[-1])))
+    here = [jnp.concatenate(held[side][:-1], axis=0) for side in range(2)]
+    near = tuple(experts(ids[:1], here[0], here[1], weights[:1]))
+    near, far_weights = lax.optimization_barrier((near, weights[1]))
+    far = tuple(experts(ids[1:], here[0], here[1], (far_weights,)))
+    near, far, last = lax.optimization_barrier((near, far, tuple(arrived[-1])))
+    early = [near[side].astype(F32) + far[side].astype(F32) for side in range(2)]
     late = experts(ids, last[0], last[1], weights)
     totals = []
     for side in range(2):
-        added = [early[side][:half].astype(F32)]
+        added = [early[side][:half]]
         waiting, low = [], half
         for level in range(n_bits - 1):
             size = half * 2**level
-            waiting.append(early[side][low : low + size].astype(F32))
+            waiting.append(early[side][low : low + size])
             low += size
         waiting.append(late[side].astype(F32))
         for level in reversed(range(n_bits)):
@@ -596,9 +599,10 @@
     far_first = lax.all_gather(far_first, "head", axis=0, tiled=True)
     back = lax.all_to_all(answers, "head", split_axis=0, concat_axis=0, tiled=True)
 
+    back, far_down = lax.optimization_barrier((back, far_down))
     router = jnp.pad(router_weight, ((0, 0), (0, LANES - router_weight.shape[1])))
     residual, sent = settle(tokens, back, w_out, norm2_gain, router, routes)
-    sent, far_second = lax.optimization_barrier((sent, far_second))
+    sent, far_first, far_second = lax.optimization_barrier((sent, far_first, far_second))
     far_second = lax.all_gather(far_second, "head", axis=0, tiled=True)
     ids = jnp.stack([req_index, req_index ^ far_mask]).astype(jnp.int32)
     weights = (((w_gate_up[0],), w_down[0]), ((far_first, far_second), far_down))

time: 232 us -> 226 us (0.974)
    ppermute x13, waiting for transfers between devices: 36.4 us -> 74.7 us  [swapped(): return lax.ppermute(value, axis, pairs)]
    all_gather x1, waiting for transfers between devices: 26.2 us -> 0.01 us  [on_device(): far_second = lax.all_gather(far_second, 'head', axis=0, tiled=True)]
    all_to_all x1, waiting for transfers between devices: 8.74 us -> 0.01 us  [on_device(): lax.all_to_all(outgoing, 'head', split_axis=0, concat_axis=0, tiled=True)]
    pallas_call x1, Pallas kernels: 16.9 us -> 13.3 us  [attend(): pl.pallas_call(attend_kernel, grid_spec=pltpu.PrefetchScalarGridSpec(num_...]
    all_gather x1, waiting for transfers between devices: 2.92 us -> 0.01 us  [on_device(): far_down = lax.all_gather(far_down, 'head', axis=0, tiled=True)]
    unnamed x38 -> x48, local copies, waits for them, and re-layouts: 3.97 us -> 6.02 us
    pallas_call x2 -> x3, Pallas kernels: 33.5 us -> 35.2 us  [experts(): pl.pallas_call(functools.partial(expert_kernel, tuple((len(pieces) for pi...]
  transfers between devices with their start and end apart: 18 -> 18, of which waited for: 8 -> 7; matrix products, arithmetic and copies ran while one was open for 8% -> 7% of each run, Pallas kernels for 22% -> 22%
where the time goes in v2:
time: 226 us; the launch traced here: 225 us
  waiting for transfers between devices  90.2 us (40%)
  Pallas kernels  69.1 us (31%)
  starting transfers between devices  20.9 us (9%)
  between operations  18.7 us (8%)
  local copies, waits for them, and re-layouts  17.1 us (8%)
  other arithmetic  9.05 us (4%)
    ppermute x13, waiting for transfers between devices, swapped(): return lax.ppermute(value, axis, pairs)  74.7 us
    pallas_call x3, Pallas kernels, experts(): pl.pallas_call(functools.partial(expert_kernel, tuple((len(pieces) for pi...  35.2 us
    all_to_all x1, waiting for transfers between devices, on_device(): lax.all_to_all(answers, 'head', split_axis=0, concat_axis=0, tiled=True)  15.5 us
    ppermute x13, starting transfers between devices, swapped(): return lax.ppermute(value, axis, pairs)  13.6 us
    pallas_call x1, Pallas kernels, attend(): pl.pallas_call(attend_kernel, grid_spec=pltpu.PrefetchScalarGridSpec(num_...  13.3 us
    pallas_call x1, Pallas kernels, project(): pl.pallas_call(functools.partial(project_kernel, n_groups), grid=(columns...  9.13 us
    pallas_call x1, Pallas kernels, settle(): pl.pallas_call(settle_kernel, grid=(n_groups,), in_specs=[whole(rows, MOD...  8.76 us
    unnamed x48, local copies, waits for them, and re-layouts  6.02 us
  transfers between devices with their start and end apart: 18, of which 7 were waited for; matrix products, arithmetic and copies ran while one was open for 7% of the time, Pallas kernels for 22%

profile of v2, /device:TPU:0, one launch (start us, length us, event | category | flops | bytes accessed | tf_op | source)
XLA Modules:
  0.0 225.0 jit_solution(6075883511175850579)
XLA Ops:
  7.9 2.0 compare_select_fusion.3
  12.6 2.7 %leaving.1 = bf16[2,8,128,128]{3,2,1,0:T(8,128)(2,1)} custom-call(s32[9]{0:T(128)} %pad_add_fusion.pages_ref, bf16[32,128,256]{2,1,0:T(8,128)(2,1)} %k_ref.3, bf16[32,128,256]{2,1,0:T(8,128)(2,1)} %v_ref.3), custom_call_target="tpu_custom_call" | custom-call | bytes 1048576 | tf_op jit(solution)/shard_map/leaving/pallas_call | solution.py:132
  15.4 3.0 %collective-permute-start = (bf16[2,8,128,128]{3,2,1,0:T(8,128)(2,1)}, bf16[2,8,128,128]{3,2,1,0:T(8,128)(2,1)}, u32[]{:S(2)}, u32[]{:S(2)}) collective-permute-start(bf16[2,8,128,128]{3,2,1,0:T(8,128)(2,1)} %leaving.1), channel_id=1, source_target_pairs={{0,4},{4,0},{8,12},{12,8},{16,20},{20,16},{24,28},{28,24},{1,5},{5... | collective-permute-start | bytes 1572872 | tf_op jit(solution)/shard_map/ppermute | solution.py:31
  24.2 9.1 %project.1 = (bf16[4,256,640]{2,1,0:T(8,128)(2,1)}, bf16[256,512]{1,0:T(8,128)(2,1)}) custom-call(bf16[256,1536]{1,0:T(8,128)(2,1)} %x_ref.1, f32[1,1536]{1,0:T(1,128)} %reshape.32.gain_ref, bf16[1536,2048]{1,0:T(8,128)(2,1)} %w_ref.2, f32[256,128]{1,0:T(8,128)} %get-tuple-element.82.cos_ref, f32[256,128]{1,0:T(8,128)} %get-tuple-element.83.sin_ref), custom_call_target="tpu_custom_call" | custom-call | flops 1610612736 | bytes 6291456 | tf_op jit(solution)/shard_map/project/pallas_call | solution.py:81
  33.3 3.5 %all-to-all-start = ((bf16[4,256,640]{2,1,0:T(8,128)(2,1)}), bf16[4,256,640]{2,1,0:T(8,128)(2,1)S(1)}, u32[]{:S(2)}, u32[]{:S(2)}) async-start(bf16[4,256,640]{2,1,0:T(8,128)(2,1)} %get-tuple-element.39), calls=%async_computation | async-start | bytes 2621440 | tf_op jit(solution)/shard_map/all_to_all | solution.py:587
  36.9 1.1 dynamic-slice_bitcast_fusion.2
  38.0 2.7 %collective-permute-start.1 = (bf16[192,1536]{1,0:T(8,128)(2,1)S(1)}, bf16[192,1536]{1,0:T(8,128)(2,1)S(1)}, u32[]{:S(2)}, u32[]{:S(2)}) collective-permute-start(bf16[192,1536]{1,0:T(8,128)(2,1)S(1)} %dynamic-slice_bitcast_fusion.2), channel_id=1, source_target_pairs={{0,16},{4,20},{8,24},{12,28},{16,0},{20,4},{24,8},{28,12},{1,17},{... | collective-permute-start | bytes 1769480 | tf_op jit(solution)/shard_map/ppermute | solution.py:31
  40.7 26.6 %collective-permute-done.1 = bf16[192,1536]{1,0:T(8,128)(2,1)S(1)} collective-permute-done((bf16[192,1536]{1,0:T(8,128)(2,1)S(1)}, bf16[192,1536]{1,0:T(8,128)(2,1)S(1)}, u32[]{:S(2)}, u32[]{:S(2)}) %collective-permute-start.1) | collective-permute-done | bytes 589856 | tf_op jit(solution)/shard_map/ppermute | solution.py:31
  68.6 2.7 %fusion.7 = (bf16[1,768,1536]{2,1,0:T(8,128)(2,1)S(1)}, bf16[1,768,1536]{2,1,0:T(8,128)(2,1)S(1)}) fusion(bf16[1,1536,1536]{2,1,0:T(8,128)(2,1)} %param.20), kind=kLoop, calls=%fused_computation.46 | loop fusion | bytes 9437184 | tf_op jit(solution)/shard_map/slice | solution.py:567
  71.5 1.1 gather_fusion
  74.6 13.3 %attend.1 = bf16[2,512,384]{2,1,0:T(8,128)(2,1)} custom-call(s32[2,16]{1,0:T(2,128)} %gather_fusion, s32[6]{0:T(128)} %pad_add_fusion.1.info_ref, bf16[2,512,640]{2,1,0:T(8,128)(2,1)} %bitcast.24, bf16[32,128,256]{2,1,0:T(8,128)(2,1)} %k_ref.3, bf16[32,128,256]{2,1,0:T(8,128)(2,1)} %v_ref.3, bf16[2,8,128,128]{3,2,1,0:T(8,128)(2,1)} %collective-permute-done.got_ref, ...), custom_call_target="tpu_custom_call" | custom-call | flops 3221225472 | bytes 4194304 | tf_op jit(solution)/shard_map/attend/pallas_call | solution.py:268
  87.9 12.8 %collective-permute-done.3 = bf16[192,1536]{1,0:T(8,128)(2,1)S(1)} collective-permute-done((bf16[192,1536]{1,0:T(8,128)(2,1)S(1)}, bf16[192,1536]{1,0:T(8,128)(2,1)S(1)}, u32[]{:S(2)}, u32[]{:S(2)}) %collective-permute-start.3) | collective-permute-done | bytes 589856 | tf_op jit(solution)/shard_map/ppermute | solution.py:31
  101.5 3.5 %all-to-all-start.1 = ((bf16[4,256,384]{2,1,0:T(8,128)(2,1)}), bf16[4,256,384]{2,1,0:T(8,128)(2,1)S(1)}, u32[]{:S(2)}, u32[]{:S(2)}) async-start(bf16[4,256,384]{2,1,0:T(8,128)(2,1)} %bitcast.25), calls=%async_computation.1 | async-start | bytes 1572864 | tf_op jit(solution)/shard_map/all_to_all | solution.py:600
  105.3 0.9 dynamic-slice_bitcast_fusion
  107.9 0.9 pad.4.router_ref
  108.8 15.5 %all-to-all-done.1.back_ref = bf16[4,256,384]{2,1,0:T(8,128)(2,1)S(1)} async-done(((bf16[4,256,384]{2,1,0:T(8,128)(2,1)}), bf16[4,256,384]{2,1,0:T(8,128)(2,1)S(1)}, u32[]{:S(2)}, u32[]{:S(2)}) %all-to-all-start.1) | async-done | bytes 786464 | tf_op jit(solution)/shard_map/all_to_all | solution.py:600
  124.3 0.9 copy-done.5
  125.1 8.8 %settle.1 = (f32[256,1536]{1,0:T(8,128)}, bf16[256,1664]{1,0:T(8,128)(2,1)}) custom-call(bf16[256,1536]{1,0:T(8,128)(2,1)} %x_ref.1, bf16[4,256,384]{2,1,0:T(8,128)(2,1)} %copy-done.5, bf16[1536,1536]{1,0:T(8,128)(2,1)} %w_ref.3, f32[1,1536]{1,0:T(1,128)} %reshape.35.gain_ref, f32[1536,128]{1,0:T(8,128)} %pad.4.router_ref, s32[256,4]{1,0:T(8,128)} %copy.19.routes_ref), custom_call_target="tpu_custom_call" | custom-call | flops 1207959552 | bytes 4718592 | tf_op jit(solution)/shard_map/settle/pallas_call | solution.py:340
  134.8 1.2 fusion.8
  136.5 11.3 %collective-permute-done.5 = bf16[128,1664]{1,0:T(8,128)(2,1)S(1)} collective-permute-done((bf16[128,1664]{1,0:T(8,128)(2,1)S(1)}, bf16[128,1664]{1,0:T(8,128)(2,1)S(1)}, u32[]{:S(2)}, u32[]{:S(2)}) %collective-permute-start.5) | collective-permute-done | bytes 426016 | tf_op jit(solution)/shard_map/ppermute | solution.py:31
  148.1 1.6 collective-permute-start.8
  150.3 9.2 %experts.3 = (bf16[256,1536]{1,0:T(8,128)(2,1)}, bf16[256,1536]{1,0:T(8,128)(2,1)}) custom-call(s32[1]{0:T(128)} %bitcast.9.ids_ref, bf16[256,1664]{1,0:T(8,128)(2,1)} %copy-done.3, bf16[256,1664]{1,0:T(8,128)(2,1)} %copy-done.4, bf16[1536,1536]{1,0:T(8,128)(2,1)} %bitcast.18, bf16[1536,1536]{1,0:T(8,128)(2,1)} %bitcast.19, bf16[768,1536]{1,0:T(8,128)(2,1)} %bitcast.22), custom_call_target="tpu_custom_call" | custom-call | flops 3623878656 | bytes 7077888 | tf_op jit(solution)/shard_map/experts/pallas_call | solution.py:454
  159.5 9.2 %experts.4 = (bf16[256,1536]{1,0:T(8,128)(2,1)}, bf16[256,1536]{1,0:T(8,128)(2,1)}) custom-call(s32[1]{0:T(128)} %bitcast.13.ids_ref, bf16[256,1664]{1,0:T(8,128)(2,1)} %copy-done.3, bf16[256,1664]{1,0:T(8,128)(2,1)} %copy-done.4, bf16[768,1536]{1,0:T(8,128)(2,1)} %all-gather.6.cloned.1.call-done.refs_0_.refs_1_.refs_3_.refs_4_, ...), custom_call_target="tpu_custom_call" | custom-call | flops 3623878656 | bytes 7077888 | tf_op jit(solution)/shard_map/experts/pallas_call | solution.py:454
  168.7 0.9 copy-done.21
  169.8 16.9 %experts.5 = (bf16[256,1536]{1,0:T(8,128)(2,1)}, bf16[256,1536]{1,0:T(8,128)(2,1)}) custom-call(s32[2]{0:T(128)} %pad_add_fusion.2.ids_ref, bf16[256,1664]{1,0:T(8,128)(2,1)} %copy-done.21, bf16[256,1664]{1,0:T(8,128)(2,1)} %copy-done.22, bf16[1536,1536]{1,0:T(8,128)(2,1)} %bitcast.20, bf16[1536,1536]{1,0:T(8,128)(2,1)} %bitcast.21, ...), custom_call_target="tpu_custom_call" | custom-call | flops 7247757312 | bytes 14155776 | tf_op jit(solution)/shard_map/experts/pallas_call | solution.py:454
  187.3 1.8 collective-permute-start.9
  189.6 16.0 %collective-permute-done.11 = bf16[256,1536]{1,0:T(8,128)(2,1)S(1)} collective-permute-done((bf16[256,1536]{1,0:T(8,128)(2,1)}, bf16[256,1536]{1,0:T(8,128)(2,1)S(1)}, u32[]{:S(2)}, u32[]{:S(2)}) %collective-permute-start.11) | collective-permute-done | bytes 786464 | tf_op jit(solution)/shard_map/ppermute | solution.py:31
  205.9 1.5 collective-permute-start.12
  207.7 1.5 collective-permute-start.10
  209.2 6.3 %collective-permute-done.12 = bf16[128,1536]{1,0:T(8,128)(2,1)S(1)} collective-permute-done((bf16[128,1536]{1,0:T(8,128)(2,1)S(1)}, bf16[128,1536]{1,0:T(8,128)(2,1)S(1)}, u32[]{:S(2)}, u32[]{:S(2)}) %collective-permute-start.12) | collective-permute-done | bytes 393248 | tf_op jit(solution)/shard_map/ppermute | solution.py:31
  215.6 1.7 collective-permute-done.10
  217.4 1.1 fusion
  (97 shorter events, 15.1 us)
Async XLA Ops:
  7.2 4.8 %copy-start = (s32[2,16]{1,0:T(2,128)S(1)}, s32[2,16]{1,0:T(2,128)}, u32[]{:S(2)}) copy-start(s32[2,16]{1,0:T(2,128)} %param.25) | copy-start | bytes 388
  12.6 5.7 %copy-start.18 = (s32[16]{0:T(128)S(1)}, s32[16]{0:T(128)}, u32[]{:S(2)}) copy-start(s32[16]{0:T(128)} %param.27) | copy-start | bytes 196
  12.6 8.3 %copy-start.2 = (s32[16]{0:T(128)S(1)}, s32[16]{0:T(128)}, u32[]{:S(2)}) copy-start(s32[16]{0:T(128)} %param.26) | copy-start | bytes 196
  12.6 9.6 %copy-start.16 = (f32[1536]{0:T(1024)S(1)}, f32[1536]{0:T(1024)}, u32[]{:S(2)}) copy-start(f32[1536]{0:T(1024)} %param.15) | copy-start | bytes 18436
  15.4 17.9 %collective-permute-start = (bf16[2,8,128,128]{3,2,1,0:T(8,128)(2,1)}, bf16[2,8,128,128]{3,2,1,0:T(8,128)(2,1)}, u32[]{:S(2)}, u32[]{:S(2)}) collective-permute-start(bf16[2,8,128,128]{3,2,1,0:T(8,128)(2,1)} %leaving.1), channel_id=1, source_target_pairs={{0,4},{4,0},{8,12},{12,8},{16,20},{20,16},{24,28},{28,24},{1,5},{5... | collective-permute-start | bytes 1572872 | tf_op jit(solution)/shard_map/ppermute | solution.py:31
  33.3 34.0 %all-to-all-start = ((bf16[4,256,640]{2,1,0:T(8,128)(2,1)}), bf16[4,256,640]{2,1,0:T(8,128)(2,1)S(1)}, u32[]{:S(2)}, u32[]{:S(2)}) async-start(bf16[4,256,640]{2,1,0:T(8,128)(2,1)} %get-tuple-element.39), calls=%async_computation | async-start | bytes 2621440 | tf_op jit(solution)/shard_map/all_to_all | solution.py:587
  36.8 87.4 %all-gather.4.cloned.1.call-start = ((), (), s32[]{:S(2)}) async-start(), calls=%async_computation.2 | async-start | bytes 2949120 | tf_op jit(solution)/shard_map/all_gather | solution.py:589
  38.0 29.3 %collective-permute-start.1 = (bf16[192,1536]{1,0:T(8,128)(2,1)S(1)}, bf16[192,1536]{1,0:T(8,128)(2,1)S(1)}, u32[]{:S(2)}, u32[]{:S(2)}) collective-permute-start(bf16[192,1536]{1,0:T(8,128)(2,1)S(1)} %dynamic-slice_bitcast_fusion.2), channel_id=1, source_target_pairs={{0,16},{4,20},{8,24},{12,28},{16,0},{20,4},{24,8},{28,12},{1,17},{... | collective-permute-start | bytes 1769480 | tf_op jit(solution)/shard_map/ppermute | solution.py:31
  68.6 65.4 %all-gather.6.cloned.1.call-start = ((), (), s32[]{:S(2)}) async-start(), calls=%async_computation.3 | async-start | bytes 2949120 | tf_op jit(solution)/shard_map/all_gather | solution.py:599
  68.6 2.9 %copy-start.20 = (s32[2]{0:T(128)S(1)}, s32[2]{0:T(128)}, u32[]{:S(2)}) copy-start(s32[2]{0:T(128)} %get-tuple-element.81) | copy-start | bytes 28
  71.2 3.4 %collective-permute-start.2 = (bf16[2,8,128,128]{3,2,1,0:T(8,128)(2,1)}, bf16[2,8,128,128]{3,2,1,0:T(8,128)(2,1)}, u32[]{:S(2)}, u32[]{:S(2)}) collective-permute-start(bf16[2,8,128,128]{3,2,1,0:T(8,128)(2,1)} %collective-permute-done.got_ref), channel_id=1, source_target_pairs={{0,1},{1,0},{2,3},{3,2},{4,5},{5,4},{6,7},{7,6},{8,9},{9,8},{10,11... | collective-permute-start | bytes 1572872 | tf_op jit(solution)/shard_map/ppermute | solution.py:31
  71.4 29.3 %collective-permute-start.3 = (bf16[192,1536]{1,0:T(8,128)(2,1)S(1)}, bf16[192,1536]{1,0:T(8,128)(2,1)S(1)}, u32[]{:S(2)}, u32[]{:S(2)}) collective-permute-start(bf16[192,1536]{1,0:T(8,128)(2,1)S(1)} %dynamic-slice_bitcast_fusion.1), channel_id=1, source_target_pairs={{0,16},{4,20},{8,24},{12,28},{16,0},{20,4},{24,8},{28,12},{1,17},{... | collective-permute-start | bytes 1769480 | tf_op jit(solution)/shard_map/ppermute | solution.py:31
  100.7 5.5 %copy-start.17 = (f32[1536]{0:T(1024)S(1)}, f32[1536]{0:T(1024)}, u32[]{:S(2)}) copy-start(f32[1536]{0:T(1024)} %param.18) | copy-start | bytes 18436
  100.7 6.1 %copy-start.15 = (f32[1536,8]{0,1:T(8,128)S(1)}, f32[1536,8]{0,1:T(8,128)}, u32[]{:S(2)}) copy-start(f32[1536,8]{0,1:T(8,128)} %param.19) | copy-start | bytes 147460
  101.5 5.5 %copy-start.19 = (s32[256,4]{0,1:T(4,128)S(1)}, s32[256,4]{0,1:T(4,128)}, u32[]{:S(2)}) copy-start(s32[256,4]{0,1:T(4,128)} %param.22) | copy-start | bytes 12292
  101.5 22.7 %all-to-all-start.1 = ((bf16[4,256,384]{2,1,0:T(8,128)(2,1)}), bf16[4,256,384]{2,1,0:T(8,128)(2,1)S(1)}, u32[]{:S(2)}, u32[]{:S(2)}) async-start(bf16[4,256,384]{2,1,0:T(8,128)(2,1)} %bitcast.25), calls=%async_computation.1 | async-start | bytes 1572864 | tf_op jit(solution)/shard_map/all_to_all | solution.py:600
  105.1 54.4 %all-gather.8.cloned.1.call-start = ((), (), s32[]{:S(2)}) async-start(), calls=%async_computation.4 | async-start | bytes 2949120 | tf_op jit(solution)/shard_map/all_gather | solution.py:606
  106.2 27.8 %collective-permute-start.4 = (bf16[192,1536]{1,0:T(8,128)(2,1)}, bf16[192,1536]{1,0:T(8,128)(2,1)S(1)}, u32[]{:S(2)}, u32[]{:S(2)}) collective-permute-start(bf16[192,1536]{1,0:T(8,128)(2,1)} %dynamic-slice_bitcast_fusion), channel_id=1, source_target_pairs={{0,16},{4,20},{8,24},{12,28},{16,0},{20,4},{24,8},{28,12},{1,17},{... | collective-permute-start | bytes 1769480 | tf_op jit(solution)/shard_map/ppermute | solution.py:31
  136.0 11.8 %collective-permute-start.5 = (bf16[128,1664]{1,0:T(8,128)(2,1)S(1)}, bf16[128,1664]{1,0:T(8,128)(2,1)S(1)}, u32[]{:S(2)}, u32[]{:S(2)}) collective-permute-start(bf16[128,1664]{1,0:T(8,128)(2,1)S(1)} %get-tuple-element.75), channel_id=1, source_target_pairs={{0,4},{4,0},{8,12},{12,8},{16,20},{20,16},{24,28},{28,24},{1,5},{5... | collective-permute-start | bytes 1277960 | tf_op jit(solution)/shard_map/ppermute | solution.py:31
  136.5 11.5 %collective-permute-start.6 = (bf16[128,1664]{1,0:T(8,128)(2,1)S(1)}, bf16[128,1664]{1,0:T(8,128)(2,1)S(1)}, u32[]{:S(2)}, u32[]{:S(2)}) collective-permute-start(bf16[128,1664]{1,0:T(8,128)(2,1)S(1)} %get-tuple-element.74), channel_id=1, source_target_pairs={{0,8},{4,12},{8,0},{12,4},{16,24},{20,28},{24,16},{28,20},{1,9},{5... | collective-permute-start | bytes 1277960 | tf_op jit(solution)/shard_map/ppermute | solution.py:31
  147.9 2.4 %copy-start.3 = (bf16[256,1664]{1,0:T(8,128)(2,1)}, bf16[256,1664]{1,0:T(8,128)(2,1)S(1)}, u32[]{:S(2)}) copy-start(bf16[256,1664]{1,0:T(8,128)(2,1)S(1)} %pad_maximum_fusion.xa_ref) | copy-start | bytes 2555908
  147.9 20.8 %collective-permute-start.7 = (bf16[256,1664]{1,0:T(8,128)(2,1)S(1)}, bf16[256,1664]{1,0:T(8,128)(2,1)S(1)}, u32[]{:S(2)}, u32[]{:S(2)}) collective-permute-start(bf16[256,1664]{1,0:T(8,128)(2,1)S(1)} %pad_maximum_fusion.xa_ref), channel_id=1, source_target_pairs={{0,8},{4,12},{8,0},{12,4},{16,24},{20,28},{24,16},{28,20},{1,9},{5... | collective-permute-start | bytes 2555912 | tf_op jit(solution)/shard_map/ppermute | solution.py:31
  148.1 2.2 copy-start.4
  148.1 20.6 %collective-permute-start.8 = (bf16[256,1664]{1,0:T(8,128)(2,1)S(1)}, bf16[256,1664]{1,0:T(8,128)(2,1)S(1)}, u32[]{:S(2)}, u32[]{:S(2)}) collective-permute-start(bf16[256,1664]{1,0:T(8,128)(2,1)S(1)} %pad_maximum_fusion.1.xb_ref), channel_id=1, source_target_pairs={{0,4},{4,0},{8,12},{12,8},{16,20},{20,16},{24,28},{28,24},{1,5},{5... | collective-permute-start | bytes 2555912 | tf_op jit(solution)/shard_map/ppermute | solution.py:31
  169.8 19.3 %copy-start.9 = (bf16[256,1536]{1,0:T(8,128)(2,1)S(1)}, bf16[256,1536]{1,0:T(8,128)(2,1)}, u32[]{:S(2)}) copy-start(bf16[256,1536]{1,0:T(8,128)(2,1)} %get-tuple-element.66) | copy-start | bytes 2359300
  169.8 19.3 %copy-start.11 = (bf16[256,1536]{1,0:T(8,128)(2,1)S(1)}, bf16[256,1536]{1,0:T(8,128)(2,1)}, u32[]{:S(2)}) copy-start(bf16[256,1536]{1,0:T(8,128)(2,1)} %get-tuple-element.67) | copy-start | bytes 2359300
  186.7 18.9 %collective-permute-start.11 = (bf16[256,1536]{1,0:T(8,128)(2,1)}, bf16[256,1536]{1,0:T(8,128)(2,1)S(1)}, u32[]{:S(2)}, u32[]{:S(2)}) collective-permute-start(bf16[256,1536]{1,0:T(8,128)(2,1)} %get-tuple-element.68), channel_id=1, source_target_pairs={{0,4},{4,0},{8,12},{12,8},{16,20},{20,16},{24,28},{28,24},{1,5},{5... | collective-permute-start | bytes 2359304 | tf_op jit(solution)/shard_map/ppermute | solution.py:31
  187.3 2.1 copy-start.8
  187.3 2.1 copy-start.10
  187.3 20.1 %collective-permute-start.9 = (bf16[256,1536]{1,0:T(8,128)(2,1)}, bf16[256,1536]{1,0:T(8,128)(2,1)S(1)}, u32[]{:S(2)}, u32[]{:S(2)}) collective-permute-start(bf16[256,1536]{1,0:T(8,128)(2,1)} %get-tuple-element.65), channel_id=1, source_target_pairs={{0,8},{4,12},{8,0},{12,4},{16,24},{20,28},{24,16},{28,20},{1,9},{5... | collective-permute-start | bytes 2359304 | tf_op jit(solution)/shard_map/ppermute | solution.py:31
  205.9 9.6 %collective-permute-start.12 = (bf16[128,1536]{1,0:T(8,128)(2,1)S(1)}, bf16[128,1536]{1,0:T(8,128)(2,1)S(1)}, u32[]{:S(2)}, u32[]{:S(2)}) collective-permute-start(bf16[128,1536]{1,0:T(8,128)(2,1)S(1)} %fusion.1), channel_id=1, source_target_pairs={{0,8},{4,12},{8,0},{12,4},{16,24},{20,28},{24,16},{28,20},{1,9},{5... | collective-permute-start | bytes 1179656 | tf_op jit(solution)/shard_map/ppermute | solution.py:31
  207.7 9.6 %collective-permute-start.10 = (bf16[128,1536]{1,0:T(8,128)(2,1)S(1)}, bf16[128,1536]{1,0:T(8,128)(2,1)S(1)}, u32[]{:S(2)}, u32[]{:S(2)}) collective-permute-start(bf16[128,1536]{1,0:T(8,128)(2,1)S(1)} %fusion.3), channel_id=1, source_target_pairs={{0,4},{4,0},{8,12},{12,8},{16,20},{20,16},{24,28},{28,24},{1,5},{5... | collective-permute-start | bytes 1179656 | tf_op jit(solution)/shard_map/ppermute | solution.py:31
  (9 other events, 9.6 us)
Sparse Core Ops, SparseCore 0:
  68.2 24.4 all-gather.3
  101.6 29.1 all-gather.5
  134.9 23.5 all-gather.7
